TPU v7x, 128 devices: a whole 4x4x4 slice. The times are simulated.
128 devices in a mesh: outer: 32 (over x, z, core), inner: 4 (over y).
Axes of the slice: x: 4, y: 4, z: 4, core: 2. Of those that a mesh axis runs over, the one named last changes fastest.
Arguments:
- inputs: bfloat16 [16384, 4096], P(('outer', 'inner')), may hold values from -6 to 6
- log_decay: bfloat16 [16384, 64], P(('outer', 'inner')), may hold values from -1 to 0, as said below
- read_in: bfloat16 [16384, 1024], P(('outer', 'inner')), may hold values from -0.29882812 to 0.29882812
- read_out: bfloat16 [16384, 1024], P(('outer', 'inner')), may hold values from -0.29882812 to 0.29882812
- initial_state: float32 [64, 64, 128], P('inner'), may hold values from -24 to 24
- output_grad: bfloat16 [16384, 4096], P(('outer', 'inner')), may hold values from -6 to 6
Outputs:
- outputs: bfloat16 [16384, 4096], P(('outer', 'inner'))
- inputs_grad: bfloat16 [16384, 4096], P(('outer', 'inner'))
- decay_grad: bfloat16 [16384, 64], P(('outer', 'inner'))
- read_in_grad: bfloat16 [16384, 1024], P(('outer', 'inner'))
- read_out_grad: bfloat16 [16384, 1024], P(('outer', 'inner'))
- initial_grad: float32 [64, 64, 128], P('inner')
Inputs may be any that keep to these rules, and one draw needn't show every extreme that they name: log_decay is negative.
All inputs are finite; a program needn't handle non-finite values.
Results may differ from a plain program's by a relative error of at most 0.022.
Values may be sent and summed in bfloat16 or wider, within the bound.
A program may use at most 512 MiB of HBM per device.

v0:
```python
import jax
import jax.numpy as jnp
from jax import lax
from jax.sharding import PartitionSpec as P

L = 128


def carried_in(x, axis, combine, identity, reverse):
    size, here = (lax.axis_size(axis), lax.axis_index(axis))
    everything = jax.tree.map(lambda part: lax.all_gather(part, axis), x)
    start = jax.tree.map(
        lambda part, zero: jnp.broadcast_to(jnp.asarray(zero, part.dtype), part.shape), x, identity
    )

    def turn(k, before):
        at = size - 1 - k if reverse else k
        reached = at > here if reverse else at < here
        new = combine(before, jax.tree.map(lambda part: part[at], everything))
        return jax.tree.map(lambda a, b: jnp.where(reached, a, b), new, before)

    return lax.fori_loop(0, size, turn, start)


def block_advance(state, pieces):
    piece_x, piece_decay, piece_in, piece_out = pieces
    heads = state.shape[0]
    width = state.shape[1]
    depth = state.shape[2]
    length = piece_x.shape[0]
    groups = piece_in.shape[1] // depth
    ratio = heads // groups
    summed = jnp.cumsum(piece_decay.astype(jnp.float32), axis=0)
    row_index = lax.broadcasted_iota(jnp.int32, (length, length), 0)
    col_index = lax.broadcasted_iota(jnp.int32, (length, length), 1)
    causal = (row_index >= col_index)[None]
    spread = summed.T[:, :, None] - summed.T[:, None, :]
    decays = jnp.where(causal, jnp.exp(jnp.where(causal, spread, 0.0)), 0.0)
    in_rows = piece_in.reshape(length, groups, depth)
    out_rows = piece_out.reshape(length, groups, depth)
    input_rows = piece_x.reshape(length, groups, ratio, width)
    scores = jnp.einsum("tgn,sgn->gts", out_rows, in_rows, preferred_element_type=jnp.float32)
    weight_factors = (scores[:, None] * decays.reshape(groups, ratio, length, length)).astype(
        jnp.bfloat16
    )
    local_portion = jnp.einsum(
        "zkjm,mzkl->jzkl", weight_factors, input_rows, preferred_element_type=jnp.float32
    )
    state_low = state.astype(jnp.bfloat16).reshape(groups, ratio, width, depth)
    carried = jnp.einsum("tgn,grpn->tgrp", out_rows, state_low, preferred_element_type=jnp.float32)
    carried = carried * jnp.exp(summed).reshape(length, groups, ratio)[..., None]
    result = (local_portion + carried).reshape(length, heads * width).astype(jnp.bfloat16)
    to_end = jnp.exp(summed[-1:] - summed).reshape(length, groups, ratio)[..., None]
    weighted = (input_rows * to_end).astype(jnp.bfloat16)
    gained = jnp.einsum("tgrp,tgn->grpn", weighted, in_rows, preferred_element_type=jnp.float32)
    advanced = jnp.exp(summed[-1])[:, None, None] * state + gained.reshape(heads, width, depth)
    return (advanced, result)


def run_blocks(inputs, log_decay, read_in, read_out, state):
    blocks = inputs.shape[0] // L
    pieces = (
        inputs.reshape(blocks, L, inputs.shape[1]),
        log_decay.reshape(blocks, L, log_decay.shape[1]),
        read_in.reshape(blocks, L, read_in.shape[1]),
        read_out.reshape(blocks, L, read_out.shape[1]),
    )
    final, results = lax.scan(jax.checkpoint(block_advance), state, pieces)
    return (results.reshape(inputs.shape[0], inputs.shape[1]), final)


def device_totals(inputs, log_decay, read_in, heads, width, depth):
    blocks = inputs.shape[0] // L
    groups = read_in.shape[1] // depth
    ratio = heads // groups
    summed = jnp.cumsum(log_decay.astype(jnp.float32).reshape(blocks, L, heads), axis=1)
    to_end = jnp.exp(summed[:, -1:] - summed).reshape(blocks, L, groups, ratio)[..., None]
    weighted = (inputs.reshape(blocks, L, groups, ratio, width) * to_end).astype(jnp.bfloat16)
    gained = jnp.einsum(
        "ctgrp,ctgn->cgrpn",
        weighted,
        read_in.reshape(blocks, L, groups, depth),
        preferred_element_type=jnp.float32,
    ).reshape(blocks, heads, width, depth)
    factors = jnp.exp(summed[:, -1])

    def absorb(carry, items):
        total, state = carry
        factor, gain = items
        return ((total * factor, factor[:, None, None] * state + gain), None)

    start = (jnp.ones((heads,), jnp.float32), jnp.zeros((heads, width, depth), jnp.float32))
    (total, state), unused = lax.scan(absorb, start, (factors, gained))
    return (total, state)


def compose(earlier, later):
    return (later[0] * earlier[0], later[0][:, None, None] * earlier[1] + later[1])


def shards(inputs, log_decay, read_in, read_out, initial_state, output_grad):
    width = initial_state.shape[1]
    depth = initial_state.shape[2]
    mine_x, mine_grad, mine_decay, mine_in, mine_out = (
        lax.all_to_all(inputs, "inner", split_axis=1, concat_axis=0, tiled=True),
        lax.all_to_all(output_grad, "inner", split_axis=1, concat_axis=0, tiled=True),
        lax.all_to_all(log_decay, "inner", split_axis=1, concat_axis=0, tiled=True),
        lax.all_to_all(read_in, "inner", split_axis=1, concat_axis=0, tiled=True),
        lax.all_to_all(read_out, "inner", split_axis=1, concat_axis=0, tiled=True),
    )
    heads = initial_state.shape[0]
    total, gained = device_totals(mine_x, mine_decay, mine_in, heads, width, depth)
    identity = (jnp.ones((heads,), jnp.float32), jnp.zeros((heads, width, depth), jnp.float32))
    before_decay, before_state = carried_in((total, gained), "outer", compose, identity, False)
    entry = before_decay[:, None, None] * initial_state + before_state
    (results, final), pullback = jax.vjp(run_blocks, mine_x, mine_decay, mine_in, mine_out, entry)
    own_grad = pullback((mine_grad, jnp.zeros_like(final)))[4]
    unused, after_grad = carried_in((total, own_grad), "outer", compose, identity, True)
    grads = pullback((mine_grad, after_grad))
    start_grad = lax.psum(
        (before_decay[:, None, None] * own_grad).astype(jnp.bfloat16), "outer"
    ).astype(jnp.float32)
    outputs, inputs_grad, decay_grad, in_grad, out_grad = (
        lax.all_to_all(results, "inner", split_axis=0, concat_axis=1, tiled=True),
        lax.all_to_all(grads[0], "inner", split_axis=0, concat_axis=1, tiled=True),
        lax.all_to_all(grads[1], "inner", split_axis=0, concat_axis=1, tiled=True),
        lax.all_to_all(grads[2], "inner", split_axis=0, concat_axis=1, tiled=True),
        lax.all_to_all(grads[3], "inner", split_axis=0, concat_axis=1, tiled=True),
    )
    return (outputs, inputs_grad, decay_grad, in_grad, out_grad, start_grad)


def solution(mesh):
    placed = (
        P(("outer", "inner"), None),
        P(("outer", "inner"), None),
        P(("outer", "inner"), None),
        P(("outer", "inner"), None),
        P("inner", None, None),
        P(("outer", "inner"), None),
    )
    return jax.shard_map(
        shards,
        mesh=mesh,
        in_specs=placed,
        out_specs=(
            P(("outer", "inner"), None),
            P(("outer", "inner"), None),
            P(("outer", "inner"), None),
            P(("outer", "inner"), None),
            P(("outer", "inner"), None),
            P("inner", None, None),
        ),
        check_vma=False,
    )
```

profile of v0, /device:TPU:0, one launch (start us, length us, event | category | flops | bytes accessed | tf_op | source)
XLA Modules:
  0.0 478.6 jit_solution(4233574896202535282)
XLA Ops:
  7.2 4.6 all-to-all-start
  13.5 3.6 all-to-all-done
  17.1 4.1 all-to-all-start.2
  23.4 4.5 all-to-all-done.2
  27.9 3.5 all-to-all-start.1
  32.2 12.0 %all-to-all-done.1 = bf16[128,4,1024]{0,2,1:T(8,128)(2,1)S(1)} async-done(((bf16[128,4,1024]{0,2,1:T(8,128)(2,1)}), bf16[128,4,1024]{0,2,1:T(8,128)(2,1)S(1)}, u32[]{:S(2)}, u32[]{:S(2)}) %all-to-all-start.1) | async-done | bytes 1048608 | tf_op jit(solution)/shard_map/all_to_all | solution.py:105
  44.2 2.7 fusion.59
  46.9 4.8 %while.102 = (s32[]{:T(128)}, f32[16]{0:T(128)S(1)}, f32[16,64,128]{2,1,0:T(8,128)S(1)}, f32[4,16]{1,0:T(4,128)S(1)}, f32[4,16,64,128]{3,2,1,0:T(8,128)}, /*index=5*/s32[]{:T(128)}, s32[]{:T(128)}) while((s32[]{:T(128)}, f32[16]{0:T(128)S(1)}, f32[16,64,128]{2,1,0:T(8,128)S(1)}, f32[4,16]{1,0:T(4,128)S(1)}, ...), condition=%wide.region_2.3_spmd.clone, body=%wide.region_1.2_spmd.clone.sunk | while | flops 393251 | bytes 1573280 | solution.py:93
  53.4 3.4 all-to-all-start.3
  58.2 5.3 %all-to-all-done.3 = bf16[128,4,256]{0,2,1:T(8,128)(2,1)S(1)} async-done(((bf16[128,4,256]{0,2,1:T(8,128)(2,1)}), bf16[128,4,256]{0,2,1:T(8,128)(2,1)S(1)}, u32[]{:S(2)}, u32[]{:S(2)}) %all-to-all-start.3) | async-done | bytes 262176 | tf_op jit(solution)/shard_map/all_to_all | solution.py:109
  63.5 4.2 all-to-all-start.5
  68.6 10.1 %all-to-all-done.5 = bf16[128,4,1024]{0,2,1:T(8,128)(2,1)} async-done(((bf16[128,4,1024]{0,2,1:T(8,128)(2,1)}), bf16[128,4,1024]{0,2,1:T(8,128)(2,1)}, u32[]{:S(2)}, u32[]{:S(2)}) %all-to-all-start.5) | async-done | bytes 1048608 | tf_op jit(solution)/shard_map/all_to_all | solution.py:106
  78.7 10.0 %while.104 = (s32[]{:T(128)}, f32[16,64,128]{2,1,0:T(8,128)S(1)}, bf16[4,128,16]{2,1,0:T(8,128)(2,1)}, bf16[4,128,256]{1,2,0:T(8,128)(2,1)S(1)}, bf16[4,128,1024...) while((s32[]{:T(128)}, f32[16,64,128]{2,1,0:T(8,128)S(1)}, ...), condition=%wide.region_10.11_spmd.clone, body=%wide.region_8.10_spmd.clone.sunk | while | flops 34732036 | bytes 3666243 | solution.py:68
  91.1 64.4 %all-reduce.2 = f32[512]{0:T(512)S(1)} all-reduce(f32[512]{0:T(512)S(1)} %dynamic-update-slice), channel_id=2, replica_groups=mesh['outer'=32,'inner'=4] {'outer'}, use_global_device_ids=true, to_apply=%add.2 | all-reduce | flops 512 | bytes 4096
  155.5 39.8 %while.103 = (s32[]{:T(128)}, f32[16]{0:T(128)S(1)}, f32[16,64,128]{2,1,0:T(8,128)S(1)}, s32[]{:T(128)}, f32[32,16]{1,0:T(8,128)S(1)}, /*index=5*/f32[32,16,64,128]{3,2,1,0:T(8,128)}, s32[]{:T(128)}, s32[]{:T(128)}) while((s32[]{:T(128)}, f32[16]{0:T(128)S(1)}, f32[16,64,128]{2,1,0:T(8,128)S(1)}, s32[]{:T(128)}, ...), condition=%wide.region_4.5_spmd.clone, body=%wide.region_3.4_spmd.clone.sunk | while | flops 524340 | bytes 1573299 | solution.py:22
  198.4 20.4 %while.101 = (s32[]{:T(128)}, f32[16,64,128]{2,1,0:T(8,128)S(1)}, bf16[4,128,1024]{1,2,0:T(8,128)(2,1)}, f32[4,16,64,128]{3,2,1,0:T(8,128)}, bf16[4,128,16]{2,1,...) while((s32[]{:T(128)}, f32[16,64,128]{2,1,0:T(8,128)S(1)}, ...), condition=%wide.region_7.8_spmd.clone.clone, body=%wide.region_5.7_spmd.clone.clone.sunk | while | flops 111806464 | bytes 7468605 | solution.py:68
  218.8 39.2 %while.105 = (s32[]{:T(128)}, f32[16,64,128]{2,1,0:T(8,128)S(1)}, s32[]{:T(128)}, f32[32,16]{1,0:T(8,128)S(1)}, f32[32,16,64,128]{3,2,1,0:T(8,128)}, /*index=5*/s32[]{:T(128)}, s32[]{:T(128)}, s32[]{:T(128)}, s32[]{:T(128)}) while((s32[]{:T(128)}, f32[16,64,128]{2,1,0:T(8,128)S(1)}, s32[]{:T(128)}, f32[32,16]{1,0:T(8,128)S(1)}, ...), condition=%wide.region_12.13_spmd.clone, body=%wide.region_11.12_spmd.clone.sunk | while | flops 524296 | bytes 1573223 | solution.py:22
  261.2 53.1 %while.100 = (s32[]{:T(128)}, f32[16,64,128]{2,1,0:T(8,128)S(1)}, bf16[4,128,1024]{1,2,0:T(8,128)(2,1)}, bf16[4,128,16]{1,2,0:T(8,128)(2,1)}, bf16[4,128,256]{1,...) while((s32[]{:T(128)}, f32[16,64,128]{2,1,0:T(8,128)S(1)}, ...), condition=%wide.region_23.24_spmd, body=%wide.region_13.23_spmd.sunk | while | flops 268662784 | bytes 21816724 | solution.py:68
  314.3 8.6 %all_to_all.160 = bf16[4,128,16]{1,2,0:T(8,128)(2,1)S(1)} all-to-all(bf16[4,128,16]{1,2,0:T(8,128)(2,1)} %get-tuple-element.752), channel_id=1, replica_groups=mesh['outer'=32,'inner'=4] {'inner'}, dimensions={0} | all-to-all | bytes 32768 | tf_op jit(solution)/shard_map/all_to_all | solution.py:126
  322.9 10.1 %all_to_all.161 = bf16[4,128,256]{1,2,0:T(8,128)(2,1)S(1)} all-to-all(bf16[4,128,256]{1,2,0:T(8,128)(2,1)} %get-tuple-element.753), channel_id=1, replica_groups=mesh['outer'=32,'inner'=4] {'inner'}, dimensions={0} | all-to-all | bytes 524288 | tf_op jit(solution)/shard_map/all_to_all | solution.py:127
  332.9 10.1 %all_to_all.162 = bf16[4,128,256]{1,2,0:T(8,128)(2,1)S(1)} all-to-all(bf16[4,128,256]{1,2,0:T(8,128)(2,1)} %get-tuple-element.754), channel_id=1, replica_groups=mesh['outer'=32,'inner'=4] {'inner'}, dimensions={0} | all-to-all | bytes 524288 | tf_op jit(solution)/shard_map/all_to_all | solution.py:128
  343.0 15.8 %all_to_all.163 = bf16[4,128,1024]{1,2,0:T(8,128)(2,1)S(1)} all-to-all(bf16[4,128,1024]{1,2,0:T(8,128)(2,1)} %get-tuple-element.751), channel_id=1, replica_groups=mesh['outer'=32,'inner'=4] {'inner'}, dimensions={0} | all-to-all | bytes 2097152 | tf_op jit(solution)/shard_map/all_to_all | solution.py:125
  358.8 3.5 all-to-all-start.4
  363.1 102.2 %all-reduce.5.cloned.1.call-done = bf16[16,64,128]{2,1,0:T(8,128)(2,1)} async-done(((bf16[16,64,128]{2,1,0:T(8,128)(2,1)}), bf16[16,64,128]{2,1,0:T(8,128)(2,1)}) %all-reduce.5.cloned.1.call-update) | async-done | bytes 262160 | tf_op jit(solution)/shard_map/psum | solution.py:120
  (473 shorter events, 188.0 us)
Async XLA Ops:
  7.2 9.9 %all-to-all-start = ((bf16[128,4,16]{0,2,1:T(8,128)(2,1)}), bf16[128,4,16]{0,2,1:T(8,128)(2,1)S(1)}, u32[]{:S(2)}, u32[]{:S(2)}) async-start(bf16[128,4,16]{0,2,1:T(8,128)(2,1)} %bitcast.478), calls=%async_computation | async-start | bytes 32768 | tf_op jit(solution)/shard_map/all_to_all | solution.py:107
  17.1 10.8 %all-to-all-start.2 = ((bf16[128,4,256]{0,2,1:T(8,128)(2,1)}), bf16[128,4,256]{0,2,1:T(8,128)(2,1)}, u32[]{:S(2)}, u32[]{:S(2)}) async-start(bf16[128,4,256]{0,2,1:T(8,128)(2,1)} %bitcast.51), calls=%async_computation.2 | async-start | bytes 524288 | tf_op jit(solution)/shard_map/all_to_all | solution.py:108
  27.9 16.3 %all-to-all-start.1 = ((bf16[128,4,1024]{0,2,1:T(8,128)(2,1)}), bf16[128,4,1024]{0,2,1:T(8,128)(2,1)S(1)}, u32[]{:S(2)}, u32[]{:S(2)}) async-start(bf16[128,4,1024]{0,2,1:T(8,128)(2,1)} %bitcast.47), calls=%async_computation.1 | async-start | bytes 2097152 | tf_op jit(solution)/shard_map/all_to_all | solution.py:105
  31.4 124.1 %all-gather.6.cloned.1.call-start = ((), (), s32[]{:S(2)}) async-start(), calls=%async_computation.11 | async-start | bytes 17301504 | tf_op jit(solution)/shard_map/all_gather | solution.py:11
  46.9 5.7 %copy-start.7 = (bf16[128,1024]{1,0:T(8,128)(2,1)S(1)}, bf16[128,1024]{1,0:T(8,128)(2,1)}, u32[]{:S(2)}) copy-start(bf16[128,1024]{1,0:T(8,128)(2,1)} %param.21) | copy-start | bytes 786436
  51.8 5.1 %copy-start.5 = (bf16[128,4096]{1,0:T(8,128)(2,1)S(1)}, bf16[128,4096]{1,0:T(8,128)(2,1)}, u32[]{:S(2)}) copy-start(bf16[128,4096]{1,0:T(8,128)(2,1)} %param.23) | copy-start | bytes 3145732
  53.4 10.1 %all-to-all-start.3 = ((bf16[128,4,256]{0,2,1:T(8,128)(2,1)}), bf16[128,4,256]{0,2,1:T(8,128)(2,1)S(1)}, u32[]{:S(2)}, u32[]{:S(2)}) async-start(bf16[128,4,256]{0,2,1:T(8,128)(2,1)} %bitcast.58), calls=%async_computation.3 | async-start | bytes 524288 | tf_op jit(solution)/shard_map/all_to_all | solution.py:109
  63.5 15.2 %all-to-all-start.5 = ((bf16[128,4,1024]{0,2,1:T(8,128)(2,1)}), bf16[128,4,1024]{0,2,1:T(8,128)(2,1)}, u32[]{:S(2)}, u32[]{:S(2)}) async-start(bf16[128,4,1024]{0,2,1:T(8,128)(2,1)} %bitcast.62), calls=%async_computation.5 | async-start | bytes 2097152 | tf_op jit(solution)/shard_map/all_to_all | solution.py:106
  67.7 151.0 %all-gather.8.cloned.1.call-start = ((), (), s32[]{:S(2)}) async-start(), calls=%async_computation.12 | async-start | bytes 17301504 | tf_op jit(solution)/shard_map/all_gather | solution.py:11
  78.7 10.9 %copy-start.8 = (u32[128]{0:T(128)S(1)}, u32[128]{0:T(128)}, u32[]{:S(2)}) copy-start(u32[128]{0:T(128)} %constant.236) | copy-start | bytes 1540
  155.5 39.8 %copy-start.1 = (f32[16,64,128]{2,1,0:T(8,128)S(1)}, f32[16,64,128]{2,1,0:T(8,128)}, u32[]{:S(2)}) copy-start(f32[16,64,128]{2,1,0:T(8,128)} %copy-done) | copy-start | bytes 1572868
  261.2 1.2 copy-start.2
  266.5 0.9 copy-start.6
  270.6 3.9 copy-start.3
  274.5 1.2 copy-start.2
  279.8 0.9 copy-start.6
  283.9 3.9 copy-start.3
  287.8 1.2 copy-start.2
  293.1 0.9 copy-start.6
  297.2 3.9 copy-start.3
  301.0 1.2 copy-start.2
  310.4 3.9 copy-start.3
  358.8 111.3 %all-to-all-start.4 = ((bf16[4,128,1024]{1,2,0:T(8,128)(2,1)}), bf16[4,128,1024]{1,2,0:T(8,128)(2,1)S(1)}, u32[]{:S(2)}, u32[]{:S(2)}) async-start(bf16[4,128,1024]{1,2,0:T(8,128)(2,1)} %get-tuple-element.747), calls=%async_computation.4 | async-start | bytes 2097152 | tf_op jit(solution)/shard_map/all_to_all | solution.py:124
  362.4 103.0 %all-reduce.5.cloned.1.call-start = ((), (), s32[]{:S(2)}) async-start(), calls=%async_computation.10 | async-start | bytes 524288 | tf_op jit(solution)/shard_map/psum | solution.py:120
  (3 other events, 2.5 us)
Sparse Core Ops, SparseCore 0:
  52.7 73.3 all-gather.5
  128.9 72.2 all-gather.7
  367.0 98.2 all-reduce.4
where the time goes:
time: 485 us; the launch traced here: 479 us
  waiting for transfers between devices  138 us (28%)
  blocking collectives  109 us (22%)
  other arithmetic  98.6 us (20%)
  local copies, waits for them, and re-layouts  66.8 us (14%)
  matrix products  24.6 us (5%)
  starting transfers between devices  23.4 us (5%)
  between operations  14.7 us (3%)
    psum x1, waiting for transfers between devices, shards(): lax.psum((before_decay[:, None, None] * own_grad).astype(jnp.bfloat16), '...  102 us
    select_n x96, other arithmetic, turn(): return jax.tree.map(lambda a, b: jnp.where(reached, a, b), new, before)  76.6 us
    unnamed x1, blocking collectives  64.4 us
    squeeze x24, local copies, waits for them, and re-layouts, run_blocks(): final, results = lax.scan(jax.checkpoint(block_advance), state, pieces)  18.3 us
    dynamic_update_slice x28, local copies, waits for them, and re-layouts, run_blocks(): final, results = lax.scan(jax.checkpoint(block_advance), state, pieces)  17.1 us
    all_to_all x1, blocking collectives, shards(): lax.all_to_all(grads[0], 'inner', split_axis=0, concat_axis=1, tiled=True)  15.8 us
    all_to_all x1, waiting for transfers between devices, shards(): lax.all_to_all(inputs, 'inner', split_axis=1, concat_axis=0, tiled=True)  12 us
    dot_general x12, matrix products, block_advance(): jnp.einsum('zkjm,mzkl->jzkl', weight_factors, input_rows, preferred_eleme...  11 us
  transfers between devices with their start and end apart: 9, of which 6 were waited for; matrix products, arithmetic and copies ran while one was open for 18% of the time, Pallas kernels for 0%

commit v1 on v0

v1 whole, which is shorter than its diff:
```python
import functools

import jax
import jax.numpy as jnp
from jax import lax
from jax.experimental import pallas as pl
from jax.experimental.pallas import tpu as pltpu
from jax.sharding import PartitionSpec as P

F32 = jnp.float32
BF16 = jnp.bfloat16
NN = ((1,), (0,))
NT = ((1,), (1,))
TN = ((0,), (0,))
MESH = pl.DeviceIdType.MESH


def dot(a, b, dims):
    return lax.dot_general(a, b, (dims, ((), ())), preferred_element_type=F32)


def exact_dot(a, b, dims):
    return lax.dot_general(
        a, b, (dims, ((), ())), preferred_element_type=F32, precision=lax.Precision.HIGHEST
    )


def split_dot(a, b, dims):
    high = a.astype(BF16)
    low = (a - high.astype(F32)).astype(BF16)
    return dot(high, b, dims) + dot(low, b, dims)


def iota(shape, axis):
    return lax.broadcasted_iota(jnp.int32, shape, axis)


def as_bf16(mask):
    return jnp.where(mask, 1.0, 0.0).astype(BF16)


def lower(length):
    return as_bf16(iota((length, length), 0) >= iota((length, length), 1))


def spread_sums(decay_ref, group, ratio, width):
    length, heads = decay_ref.shape
    columns = ratio * width
    pick = as_bf16(iota((heads, columns), 0) == group * ratio + iota((heads, columns), 1) // width)
    return dot(lower(length), dot(decay_ref[...], pick, NN).astype(BF16), NN)


def head_decays(decay_ref, group, ratio):
    length, heads = decay_ref.shape
    pick = as_bf16(iota((heads, ratio), 0) == group * ratio + iota((heads, ratio), 1))
    return dot(decay_ref[...], pick, NN).astype(BF16)


def gains_kernel(ratio, width, x_ref, decay_ref, in_ref, out_ref, grad_ref, gain_ref, own_ref, total_ref):
    group = pl.program_id(0)
    length = x_ref.shape[0]
    summed = spread_sums(decay_ref, group, ratio, width)
    weighted = (x_ref[...].astype(F32) * jnp.exp(summed[length - 1 :] - summed)).astype(BF16)
    gain_ref[...] = dot(weighted, in_ref[...], TN).astype(BF16)
    scaled = (grad_ref[...].astype(F32) * jnp.exp(summed)).astype(BF16)
    own_ref[...] = dot(scaled, out_ref[...], TN).astype(BF16)
    total_ref[...] = dot(head_decays(decay_ref, group, ratio), jnp.ones((length, 128), BF16), TN)


def gains(x, decay, read_in, read_out, grad, heads, width, depth):
    length = x.shape[0]
    groups = read_in.shape[1] // depth
    ratio = heads // groups
    columns = ratio * width
    wide = pl.BlockSpec((length, columns), lambda g: (0, g))
    narrow = pl.BlockSpec((length, depth), lambda g: (0, g))
    state = pl.BlockSpec((columns, depth), lambda g: (g, 0))
    return pl.pallas_call(
        functools.partial(gains_kernel, ratio, width),
        grid=(groups,),
        in_specs=[wide, pl.BlockSpec((length, heads), lambda g: (0, 0)), narrow, narrow, wide],
        out_specs=[state, state, pl.BlockSpec((ratio, 128), lambda g: (g, 0))],
        out_shape=[
            jax.ShapeDtypeStruct((heads * width, depth), BF16),
            jax.ShapeDtypeStruct((heads * width, depth), BF16),
            jax.ShapeDtypeStruct((heads, 128), F32),
        ],
        name="gains",
    )(x, decay, read_in, read_out, grad)


def carry_kernel(
    n_outer,
    n_inner,
    width,
    gain_ref,
    own_ref,
    total_ref,
    init_ref,
    state_ref,
    after_ref,
    start_ref,
    total1,
    gain1,
    own1,
    send_total,
    total2,
    send_gain,
    gain2,
    send_own,
    own2,
    send_before,
    before,
    send_behind,
    behind,
    send_state,
    send_after,
    inner_send,
    inner_recv,
    outer_send,
    outer_recv,
):
    outer = lax.axis_index("outer")
    inner = lax.axis_index("inner")
    heads = total1.shape[1]
    rows = gain2.shape[1]

    def inner_copy(stage, k, src, dst):
        to = lax.rem(inner + k, n_inner)
        return pltpu.make_async_remote_copy(
            src_ref=src.at[to],
            dst_ref=dst.at[inner],
            send_sem=inner_send.at[stage, k],
            recv_sem=inner_recv.at[stage, k],
            device_id=(outer, to),
            device_id_type=MESH,
        )

    def outer_copy(stage, k, src, dst):
        to = lax.rem(outer + k, n_outer)
        return pltpu.make_async_remote_copy(
            src_ref=src.at[to],
            dst_ref=dst.at[outer],
            send_sem=outer_send.at[stage, k],
            recv_sem=outer_recv.at[stage, k],
            device_id=(to, inner),
            device_id_type=MESH,
        )

    def each(n, act):
        def body(k, none):
            act(k)
            return none

        lax.fori_loop(1, n, body, 0)

    def start_inner(stage, src, dst):
        each(n_inner, lambda k: inner_copy(stage, k, src, dst).start())
        dst[inner] = src[inner]

    def recv_inner(stage, src, dst):
        each(n_inner, lambda k: inner_copy(stage, k, src, dst).wait_recv())

    def sent_inner(stage, src, dst):
        each(n_inner, lambda k: inner_copy(stage, k, src, dst).wait_send())

    def start_outer(stage, src, dst):
        each(n_outer, lambda k: outer_copy(stage, k, src, dst).start())
        dst[outer] = src[outer]

    def recv_outer(stage, src, dst):
        each(n_outer, lambda k: outer_copy(stage, k, src, dst).wait_recv())

    def sent_outer(stage, src, dst):
        each(n_outer, lambda k: outer_copy(stage, k, src, dst).wait_send())

    barrier = pltpu.get_barrier_semaphore()
    each(
        n_inner,
        lambda k: pl.semaphore_signal(
            barrier, inc=1, device_id=(outer, lax.rem(inner + k, n_inner)), device_id_type=MESH
        ),
    )
    each(
        n_outer,
        lambda k: pl.semaphore_signal(
            barrier, inc=1, device_id=(lax.rem(outer + k, n_outer), inner), device_id_type=MESH
        ),
    )
    pl.semaphore_wait(barrier, n_inner + n_outer - 2)

    start_inner(0, total_ref, total1)
    start_inner(1, gain_ref, gain1)
    recv_inner(0, total_ref, total1)

    def all_decay(k, none):
        head = k * rows // width
        row = total1[0, pl.ds(head, 1), :]
        for e in range(1, n_inner):
            row = row + total1[e, pl.ds(head, 1), :]
        send_total[k] = jnp.broadcast_to(row, send_total.shape[1:])
        return none

    lax.fori_loop(0, n_outer, all_decay, 0)
    start_outer(0, send_total, total2)

    sent_inner(1, gain_ref, gain1)
    start_inner(2, own_ref, own1)
    recv_inner(1, gain_ref, gain1)

    per_head = width // rows

    def factor(e, head):
        return jnp.exp(total1[e, pl.ds(head, 1), :])

    def group_gain(head, none):
        at = pl.ds(pl.multiple_of(head * width, width), width)
        value = gain1[0, at, :].astype(F32)
        for e in range(1, n_inner):
            value = factor(e, head) * value + gain1[e, at, :].astype(F32)
        value = value.astype(BF16)
        for i in range(per_head):
            send_gain[head * per_head + i] = value[i * rows : (i + 1) * rows]
        return none

    lax.fori_loop(0, heads, group_gain, 0)
    start_outer(1, send_gain, gain2)
    recv_outer(0, send_total, total2)
    recv_outer(1, send_gain, gain2)

    def scan_before(o, value):
        send_before[o] = value.astype(BF16)
        return jnp.exp(total2[o][0:1]) * value + gain2[o].astype(F32)

    lax.fori_loop(
        0, n_outer, scan_before, init_ref[pl.ds(pl.multiple_of(outer * rows, rows), rows), :]
    )
    start_outer(3, send_before, before)

    recv_inner(2, own_ref, own1)

    def group_own(head, none):
        at = pl.ds(pl.multiple_of(head * width, width), width)
        value = own1[n_inner - 1, at, :].astype(F32)
        for e in range(n_inner - 2, -1, -1):
            value = factor(e, head) * value + own1[e, at, :].astype(F32)
        value = value.astype(BF16)
        for i in range(per_head):
            send_own[head * per_head + i] = value[i * rows : (i + 1) * rows]
        return none

    lax.fori_loop(0, heads, group_own, 0)
    start_outer(2, send_own, own2)

    recv_outer(3, send_before, before)

    def block_states(head, none):
        at = pl.ds(pl.multiple_of(head * width, width), width)
        value = jnp.concatenate(
            [before[head * per_head + i].astype(F32) for i in range(per_head)], axis=0
        )
        for e in range(n_inner):
            send_state[e, at, :] = value.astype(BF16)
            if e < n_inner - 1:
                value = factor(e, head) * value + gain1[e, at, :].astype(F32)
        return none

    lax.fori_loop(0, heads, block_states, 0)
    start_inner(3, send_state, state_ref)

    recv_outer(2, send_own, own2)

    def scan_behind(i, value):
        o = n_outer - 1 - i
        send_behind[o, 0:rows, :] = value.astype(BF16)
        return jnp.exp(total2[o][0:1]) * value + own2[o].astype(F32)

    first = lax.fori_loop(0, n_outer, scan_behind, jnp.zeros(own2.shape[1:], F32)).astype(BF16)

    def add_first(o, none):
        send_behind[o, rows:, :] = first
        return none

    lax.fori_loop(0, n_outer, add_first, 0)
    start_outer(4, send_behind, behind)
    recv_outer(4, send_behind, behind)

    def block_after(head, none):
        at = pl.ds(pl.multiple_of(head * width, width), width)
        value = jnp.concatenate(
            [behind[head * per_head + i, 0:rows, :].astype(F32) for i in range(per_head)], axis=0
        )
        for e in range(n_inner - 1, -1, -1):
            send_after[e, at, :] = value.astype(BF16)
            if e > 0:
                value = factor(e, head) * value + own1[e, at, :].astype(F32)
        return none

    lax.fori_loop(0, heads, block_after, 0)
    start_inner(4, send_after, after_ref)

    def put_first(k, none):
        start_ref[k] = behind[k, rows:, :]
        return none

    lax.fori_loop(0, n_outer, put_first, 0)

    recv_inner(3, send_state, state_ref)
    recv_inner(4, send_after, after_ref)
    sent_inner(0, total_ref, total1)
    sent_inner(2, own_ref, own1)
    sent_inner(3, send_state, state_ref)
    sent_inner(4, send_after, after_ref)
    sent_outer(0, send_total, total2)
    sent_outer(1, send_gain, gain2)
    sent_outer(2, send_own, own2)
    sent_outer(3, send_before, before)
    sent_outer(4, send_behind, behind)


def carry(gain, own, total, init, n_outer, n_inner, width, depth):
    all_rows = gain.shape[0]
    chunk = all_rows // n_inner
    rows = chunk // n_outer
    heads = chunk // width
    vmem = pl.BlockSpec(memory_space=pltpu.VMEM)
    chunks = (n_inner, chunk, depth)
    pieces = (n_outer, rows, depth)
    doubles = (n_outer, 2 * rows, depth)
    totals = (n_outer, 8, depth)
    return pl.pallas_call(
        functools.partial(carry_kernel, n_outer, n_inner, width),
        in_specs=[vmem] * 4,
        out_specs=[vmem] * 3,
        out_shape=[
            jax.ShapeDtypeStruct(chunks, BF16),
            jax.ShapeDtypeStruct(chunks, BF16),
            jax.ShapeDtypeStruct(pieces, BF16),
        ],
        scratch_shapes=[
            pltpu.VMEM((n_inner, heads, depth), F32),
            pltpu.VMEM(chunks, BF16),
            pltpu.VMEM(chunks, BF16),
            pltpu.VMEM(totals, F32),
            pltpu.VMEM(totals, F32),
            pltpu.VMEM(pieces, BF16),
            pltpu.VMEM(pieces, BF16),
            pltpu.VMEM(pieces, BF16),
            pltpu.VMEM(pieces, BF16),
            pltpu.VMEM(pieces, BF16),
            pltpu.VMEM(pieces, BF16),
            pltpu.VMEM(doubles, BF16),
            pltpu.VMEM(doubles, BF16),
            pltpu.VMEM(chunks, BF16),
            pltpu.VMEM(chunks, BF16),
            pltpu.SemaphoreType.DMA((5, n_inner)),
            pltpu.SemaphoreType.DMA((5, n_inner)),
            pltpu.SemaphoreType.DMA((5, n_outer)),
            pltpu.SemaphoreType.DMA((5, n_outer)),
        ],
        compiler_params=pltpu.CompilerParams(
            collective_id=0, has_side_effects=True, vmem_limit_bytes=40 * 2**20
        ),
        name="carry",
    )(
        gain.reshape(chunks),
        own.reshape(chunks),
        total.reshape(n_inner, heads, depth),
        init,
    )


def block_kernel(
    ratio,
    width,
    x_ref,
    decay_ref,
    in_ref,
    out_ref,
    grad_ref,
    state_ref,
    after_ref,
    start_ref,
    y_ref,
    dx_ref,
    ddecay_ref,
    din_ref,
    dout_ref,
    dstart_ref,
    upper_sum,
    lower_sum,
    state_sum,
):
    group = pl.program_id(0)
    length = x_ref.shape[0]
    heads = decay_ref.shape[1]
    columns = ratio * width
    dstart_ref[...] = start_ref[...].astype(F32)

    summed = spread_sums(decay_ref, group, ratio, width)
    from_start = jnp.exp(summed)
    to_end = jnp.exp(summed[length - 1 :] - summed)
    picked = head_decays(decay_ref, group, ratio)
    low = lower(length)
    down = dot(low, picked, NN)
    across = dot(picked, low, ((0,), (1,)))
    x = x_ref[...]
    grad = grad_ref[...]
    x32 = x.astype(F32)
    grad32 = grad.astype(F32)
    b = in_ref[...]
    c = out_ref[...]
    state = state_ref[...]
    after = after_ref[...]
    scores = dot(c, b, NT)
    causal = iota((length, length), 0) >= iota((length, length), 1)

    local = []
    local_dx = []
    dscores = jnp.zeros((length, length), F32)
    for r in range(ratio):
        gap = down[:, r : r + 1] - across[r : r + 1, :]
        decays = jnp.exp(jnp.where(causal, gap, -1e30))
        weights = (scores * decays).astype(BF16)
        at = slice(r * width, (r + 1) * width)
        local.append(dot(weights, x[:, at], NN))
        local_dx.append(dot(weights, grad[:, at], TN))
        dscores = dscores + dot(grad[:, at], x[:, at], NT) * decays
    y = jnp.concatenate(local, axis=1) + dot(c, state, NT) * from_start
    y_ref[...] = y.astype(BF16)
    near_dx = jnp.concatenate(local_dx, axis=1)
    far_dx = dot(b, after, NT) * to_end
    dx_ref[...] = (near_dx + far_dx).astype(BF16)

    dscores = dscores.astype(BF16)
    dout_ref[...] = (
        dot(dscores, b, NN) + dot((grad32 * from_start).astype(BF16), state, NN)
    ).astype(BF16)
    din_ref[...] = (dot(dscores, c, TN) + dot((x32 * to_end).astype(BF16), after, NN)).astype(BF16)

    place = as_bf16(iota((columns, heads), 1) == group * ratio + iota((columns, heads), 0) // width)
    up = split_dot(y * grad32 - x32 * near_dx, place, NN)
    lo = split_dot(x32 * far_dx, place, NN)
    product = state.astype(F32) * after.astype(F32)
    total = dot(picked, jnp.ones((length, product.shape[1]), BF16), TN)
    state_sum[pl.ds(pl.multiple_of(group * ratio, ratio), ratio), :] = (
        jnp.sum(product.reshape(ratio, width, product.shape[1]), axis=1) * jnp.exp(total)
    )

    @pl.when(group == 0)
    def _():
        upper_sum[...] = up
        lower_sum[...] = lo

    @pl.when(group > 0)
    def _():
        upper_sum[...] += up
        lower_sum[...] += lo

    @pl.when(group == pl.num_programs(0) - 1)
    def _():
        row = iota((length, length), 0)
        column = iota((length, length), 1)
        up_mask = jnp.where(column >= row, 1.0, 0.0)
        low_mask = jnp.where(column < row, 1.0, 0.0)
        ones = jnp.ones((length, state_sum.shape[1]), F32)
        ddecay_ref[...] = (
            exact_dot(up_mask, upper_sum[...], NN)
            + exact_dot(low_mask, lower_sum[...], NN)
            + exact_dot(ones, state_sum[...], NT)
        ).astype(BF16)


def block(x, decay, read_in, read_out, grad, state, after, start, heads, width, depth):
    length = x.shape[0]
    groups = read_in.shape[1] // depth
    ratio = heads // groups
    columns = ratio * width
    share = start.shape[0] // groups
    wide = pl.BlockSpec((length, columns), lambda g: (0, g))
    narrow = pl.BlockSpec((length, depth), lambda g: (0, g))
    tall = pl.BlockSpec((columns, depth), lambda g: (g, 0))
    part = pl.BlockSpec((share, depth), lambda g: (g, 0))
    whole = pl.BlockSpec((length, heads), lambda g: (0, 0))
    return pl.pallas_call(
        functools.partial(block_kernel, ratio, width),
        grid=(groups,),
        in_specs=[wide, whole, narrow, narrow, wide, tall, tall, part],
        out_specs=[wide, wide, whole, narrow, narrow, part],
        out_shape=[
            jax.ShapeDtypeStruct(x.shape, BF16),
            jax.ShapeDtypeStruct(x.shape, BF16),
            jax.ShapeDtypeStruct(decay.shape, BF16),
            jax.ShapeDtypeStruct(read_in.shape, BF16),
            jax.ShapeDtypeStruct(read_out.shape, BF16),
            jax.ShapeDtypeStruct(start.shape, F32),
        ],
        scratch_shapes=[
            pltpu.VMEM((length, heads), F32),
            pltpu.VMEM((length, heads), F32),
            pltpu.VMEM((heads, depth), F32),
        ],
        name="block",
    )(x, decay, read_in, read_out, grad, state, after, start)


def shards(inputs, log_decay, read_in, read_out, initial_state, output_grad):
    n_outer, n_inner = lax.axis_size("outer"), lax.axis_size("inner")
    own_heads, width, depth = initial_state.shape
    heads = own_heads * n_inner
    gain, own, total = gains(
        inputs, log_decay, read_in, read_out, output_grad, heads, width, depth
    )
    state, after, start = carry(
        gain, own, total, initial_state.reshape(-1, depth), n_outer, n_inner, width, depth
    )
    y, dx, ddecay, din, dout, dstart = block(
        inputs,
        log_decay,
        read_in,
        read_out,
        output_grad,
        state.reshape(-1, depth),
        after.reshape(-1, depth),
        start.reshape(-1, depth),
        heads,
        width,
        depth,
    )
    return (y, dx, ddecay, din, dout, dstart.reshape(initial_state.shape))


def solution(mesh):
    tokens = P(("outer", "inner"), None)
    held = P("inner", None, None)
    return jax.shard_map(
        shards,
        mesh=mesh,
        in_specs=(tokens, tokens, tokens, tokens, held, tokens),
        out_specs=(tokens, tokens, tokens, tokens, tokens, held),
        check_vma=False,
    )
```

time: 485 us -> 102 us (0.21)
  waiting for transfers between devices: 138 us -> 0 us
  blocking collectives: 109 us -> 0 us
  other arithmetic: 98.6 us -> 0 us
  Pallas kernels: 0 us -> 90.9 us
  local copies, waits for them, and re-layouts: 66.8 us -> 8.75 us
  matrix products: 24.6 us -> 0 us
  starting transfers between devices: 23.4 us -> 0 us
  between operations: 14.7 us -> 0.66 us
    psum x1 -> x0, waiting for transfers between devices: 102 us -> none  [shards(): lax.psum((before_decay[:, None, None] * own_grad).astype(jnp.bfloat16), '...]
    pallas_call x0 -> x3, Pallas kernels: none -> 90.9 us  [the longest x1 66.5 us: carry(): pl.pallas_call(functools.partial(carry_kernel, n_outer, n_inner, width),...]
    select_n x96 -> x0, other arithmetic: 76.6 us -> none  [turn(): return jax.tree.map(lambda a, b: jnp.where(reached, a, b), new, before)]
    unnamed x1 -> x0, blocking collectives: 64.4 us -> none
    all_to_all x4 -> x0, blocking collectives: 44.5 us -> none  [the longest x1 15.8 us: shards(): lax.all_to_all(grads[0], 'inner', split_axis=0, concat_axis=1, tiled=True)]
    all_to_all x6 -> x0, waiting for transfers between devices: 35.5 us -> none  [the longest x1 12 us: shards(): lax.all_to_all(inputs, 'inner', split_axis=1, concat_axis=0, tiled=True)]
    dot_general x61 -> x0, matrix products: 24.6 us -> none  [the longest x12 11 us: block_advance(): jnp.einsum('zkjm,mzkl->jzkl', weight_factors, input_rows, preferred_eleme...]
    all_to_all x6 -> x0, starting transfers between devices: 23.3 us -> none  [the longest x1 4.56 us: shards(): lax.all_to_all(log_decay, 'inner', split_axis=1, concat_axis=0, tiled=True)]
  transfers between devices with their start and end apart: 9 -> 0, of which waited for: 6 -> 0; matrix products, arithmetic and copies ran while one was open for 18% -> 0% of each run, Pallas kernels for 0% -> 0%
where the time goes in v1:
time: 102 us; the launch traced here: 100 us
  Pallas kernels  90.9 us (89%)
  local copies, waits for them, and re-layouts  8.75 us (9%)
    pallas_call x1, Pallas kernels, carry(): pl.pallas_call(functools.partial(carry_kernel, n_outer, n_inner, width),...  66.5 us
    pallas_call x1, Pallas kernels, block(): pl.pallas_call(functools.partial(block_kernel, ratio, width), grid=(group...  15.8 us
    unnamed x16, local copies, waits for them, and re-layouts  8.75 us
    pallas_call x1, Pallas kernels, gains(): pl.pallas_call(functools.partial(gains_kernel, ratio, width), grid=(group...  8.63 us

profile of v1, /device:TPU:0, one launch (start us, length us, event | category | flops | bytes accessed | tf_op | source)
XLA Modules:
  0.0 100.3 jit_solution(6367133663774624109)
XLA Ops:
  0.6 1.4 %copy.13.decay_ref = bf16[128,64]{1,0:T(8,128)(2,1)} copy(bf16[128,64]{0,1:T(8,128)(2,1)} %param.7) | data formatting | bytes 32768 | tf_op args[1]
  2.1 0.0 copy-start.4
  2.1 8.6 %gains.1 = (bf16[4096,128]{1,0:T(8,128)(2,1)}, bf16[4096,128]{1,0:T(8,128)(2,1)}, f32[64,128]{1,0:T(8,128)}) custom-call(bf16[128,4096]{1,0:T(8,128)(2,1)} %x_ref.3, bf16[128,64]{1,0:T(8,128)(2,1)} %copy.13.decay_ref, bf16[128,1024]{1,0:T(8,128)(2,1)} %in_ref.3, bf16[128,1024]{1,0:T(8,128)(2,1)} %out_ref.3, bf16[128,4096]{1,0:T(8,128)(2,1)} %grad_ref.3), custom_call_target="tpu_custom_call" | custom-call | tf_op jit(solution)/shard_map/gains/pallas_call | solution.py:78
  10.7 0.0 copy-done.4
  10.7 0.0 copy-start.2
  10.7 1.2 %copy-done.2 = bf16[4096,128]{1,0:T(8,128)(2,1)S(1)} copy-done((bf16[4096,128]{1,0:T(8,128)(2,1)S(1)}, bf16[4096,128]{1,0:T(8,128)(2,1)}, u32[]{:S(2)}) %copy-start.2) | copy-done | bytes 1048600
  11.9 0.0 copy-start.3
  11.9 1.2 %copy-done.3 = bf16[4096,128]{1,0:T(8,128)(2,1)S(1)} copy-done((bf16[4096,128]{1,0:T(8,128)(2,1)S(1)}, bf16[4096,128]{1,0:T(8,128)(2,1)}, u32[]{:S(2)}) %copy-start.3) | copy-done | bytes 1048600
  13.1 0.0 copy-start.6
  13.1 0.8 copy-done.6
  13.9 66.5 %carry.1 = (bf16[4,1024,128]{2,1,0:T(8,128)(2,1)S(1)}, bf16[4,1024,128]{2,1,0:T(8,128)(2,1)S(1)}, bf16[32,32,128]{2,1,0:T(8,128)(2,1)S(1)}) custom-call(bf16[4,1024,128]{2,1,0:T(8,128)(2,1)S(1)} %bitcast.10, bf16[4,1024,128]{2,1,0:T(8,128)(2,1)S(1)} %bitcast.11, f32[4,16,128]{2,1,0:T(8,128)S(1)} %bitcast.14, f32[1024,128]{1,0:T(8,128)S(1)} %bitcast.12), custom_call_target="tpu_custom_call" | custom-call | tf_op jit(solution)/shard_map/carry/pallas_call | solution.py:331
  80.4 0.0 copy-start
  80.4 1.0 copy-done
  81.4 0.0 copy-start.1
  81.4 1.0 %copy-done.1 = bf16[4,1024,128]{2,1,0:T(8,128)(2,1)} copy-done((bf16[4,1024,128]{2,1,0:T(8,128)(2,1)}, bf16[4,1024,128]{2,1,0:T(8,128)(2,1)S(1)}, u32[]{:S(2)}) %copy-start.1) | copy-done | bytes 1048600
  82.4 0.0 copy-start.5
  82.4 0.7 copy-done.5
  83.1 15.8 %block.1 = (bf16[128,4096]{1,0:T(8,128)(2,1)}, bf16[128,4096]{1,0:T(8,128)(2,1)}, bf16[128,64]{1,0:T(8,128)(2,1)}, bf16[128,1024]{1,0:T(8,128)(2,1)}, bf16[128,1024]{1,0:T(8,128)(2,1)}, /*index=5*/f32[1024,128]{1,0:T(8,128)}) custom-call(bf16[128,4096]{1,0:T(8,128)(2,1)} %x_ref.3, bf16[128,64]{1,0:T(8,128)(2,1)} %copy.13.decay_ref, ...), custom_call_target="tpu_custom_call" | custom-call | tf_op jit(solution)/shard_map/block/pallas_call | solution.py:485
  98.9 1.4 %copy.14 = bf16[128,64]{0,1:T(8,128)(2,1)} copy(bf16[128,64]{1,0:T(8,128)(2,1)} %get-tuple-element.32) | data formatting | bytes 32768
Async XLA Ops:
  2.1 8.6 %copy-start.4 = (f32[16,64,128]{2,1,0:T(8,128)S(1)}, f32[16,64,128]{2,1,0:T(8,128)}, u32[]{:S(2)}) copy-start(f32[16,64,128]{2,1,0:T(8,128)} %param.10) | copy-start | bytes 1572868
  10.7 1.2 %copy-start.2 = (bf16[4096,128]{1,0:T(8,128)(2,1)S(1)}, bf16[4096,128]{1,0:T(8,128)(2,1)}, u32[]{:S(2)}) copy-start(bf16[4096,128]{1,0:T(8,128)(2,1)} %get-tuple-element.18) | copy-start | bytes 3145732
  11.9 1.2 %copy-start.3 = (bf16[4096,128]{1,0:T(8,128)(2,1)S(1)}, bf16[4096,128]{1,0:T(8,128)(2,1)}, u32[]{:S(2)}) copy-start(bf16[4096,128]{1,0:T(8,128)(2,1)} %get-tuple-element.19) | copy-start | bytes 3145732
  13.1 0.8 copy-start.6
  80.4 1.0 copy-start
  81.4 1.0 %copy-start.1 = (bf16[4,1024,128]{2,1,0:T(8,128)(2,1)}, bf16[4,1024,128]{2,1,0:T(8,128)(2,1)S(1)}, u32[]{:S(2)}) copy-start(bf16[4,1024,128]{2,1,0:T(8,128)(2,1)S(1)} %get-tuple-element.22) | copy-start | bytes 3145732
  82.4 0.7 copy-start.5

commit v2 on v1

v2 whole, which is shorter than its diff:
```python
import functools

import jax
import jax.numpy as jnp
from jax import lax
from jax.experimental import pallas as pl
from jax.experimental.pallas import tpu as pltpu
from jax.sharding import PartitionSpec as P

F32 = jnp.float32
BF16 = jnp.bfloat16
NN = ((1,), (0,))
NT = ((1,), (1,))
TN = ((0,), (0,))
MESH = pl.DeviceIdType.MESH


def dot(a, b, dims):
    return lax.dot_general(a, b, (dims, ((), ())), preferred_element_type=F32)


def exact_dot(a, b, dims):
    return lax.dot_general(
        a, b, (dims, ((), ())), preferred_element_type=F32, precision=lax.Precision.HIGHEST
    )


def split_dot(a, b, dims):
    high = a.astype(BF16)
    low = (a - high.astype(F32)).astype(BF16)
    return dot(high, b, dims) + dot(low, b, dims)


def iota(shape, axis):
    return lax.broadcasted_iota(jnp.int32, shape, axis)


def as_bf16(mask):
    return jnp.where(mask, 1.0, 0.0).astype(BF16)


def lower(length):
    return as_bf16(iota((length, length), 0) >= iota((length, length), 1))


def spread_sums(decay_ref, group, ratio, width):
    heads, length = decay_ref.shape
    columns = ratio * width
    pick = as_bf16(iota((heads, columns), 0) == group * ratio + iota((heads, columns), 1) // width)
    return dot(lower(length), dot(decay_ref[...], pick, TN).astype(BF16), NN)


def head_decays(decay_ref, group, ratio):
    heads, length = decay_ref.shape
    pick = as_bf16(iota((ratio, heads), 1) == group * ratio + iota((ratio, heads), 0))
    return dot(pick, decay_ref[...], NN).astype(BF16)


def carry_kernel(
    n_inner,
    n_low,
    n_high,
    ratio,
    width,
    x_hbm,
    decay_ref,
    in_hbm,
    out_hbm,
    grad_hbm,
    init_hbm,
    state_ref,
    after_ref,
    start_ref,
    x_ref,
    in_ref,
    out_ref,
    grad_ref,
    init_ref,
    send_total,
    total1,
    send_total2,
    total2,
    send_total3,
    total3,
    send_gain,
    gain1,
    send_own,
    own1,
    send_gain2,
    gain2,
    send_own2,
    own2,
    send_gain3,
    gain3,
    send_own3,
    own3,
    send_before,
    before,
    send_behind,
    behind,
    send_state,
    send_after,
    load_sem,
    inner_send,
    inner_recv,
    low_send,
    low_recv,
    high_send,
    high_recv,
):
    outer = lax.axis_index("outer")
    inner = lax.axis_index("inner")
    low = lax.rem(outer, n_low)
    high = lax.div(outer, n_low)
    length = x_ref.shape[0]
    depth = in_ref.shape[1] * ratio // decay_ref.shape[0]
    columns = ratio * width

    def inner_peer(k):
        return lax.rem(inner + k, n_inner)

    def low_peer(k):
        return lax.rem(low + k, n_low)

    def high_peer(k):
        return lax.rem(high + k, n_high)

    def inner_id(k):
        return (outer, inner_peer(k))

    def low_id(k):
        return (high * n_low + low_peer(k), inner)

    def high_id(k):
        return (high_peer(k) * n_low + low, inner)

    def each(n, act):
        def body(k, none):
            act(k)
            return none

        lax.fori_loop(1, n, body, 0)

    def remote(src, dst, send, recv, to):
        return pltpu.make_async_remote_copy(
            src_ref=src,
            dst_ref=dst,
            send_sem=send,
            recv_sem=recv,
            device_id=to,
            device_id_type=MESH,
        )

    def inner_copy(stage, k, src, dst, at=slice(None)):
        return remote(
            src.at[inner_peer(k), at],
            dst.at[inner, at],
            inner_send.at[stage, k],
            inner_recv.at[stage, k],
            inner_id(k),
        )

    def low_copy(stage, k, src, dst, half):
        return remote(
            src.at[half, low_peer(k)],
            dst.at[half, low],
            low_send.at[stage, k],
            low_recv.at[stage, k],
            low_id(k),
        )

    def high_copy(stage, k, src, dst, half):
        return remote(
            src.at[half],
            dst.at[half, high],
            high_send.at[stage, k],
            high_recv.at[stage, k],
            high_id(k),
        )

    def total_copy(k):
        return remote(
            send_total.at[inner_peer(k)],
            total1.at[inner],
            inner_send.at[0, k],
            inner_recv.at[0, k],
            inner_id(k),
        )

    def total2_copy(k):
        return remote(
            send_total2, total2.at[low], low_send.at[0, k], low_recv.at[0, k], low_id(k)
        )

    def total3_copy(k):
        return remote(
            send_total3, total3.at[high], high_send.at[0, k], high_recv.at[0, k], high_id(k)
        )

    loads = [
        pltpu.make_async_copy(src, dst, load_sem.at[i])
        for i, (src, dst) in enumerate(
            ((x_hbm, x_ref), (in_hbm, in_ref), (grad_hbm, grad_ref), (out_hbm, out_ref))
        )
    ]
    for half in range(2):
        rows = pl.ds(pl.multiple_of((half * ratio + low) * width, width), width)
        loads.append(
            pltpu.make_async_copy(init_hbm.at[rows], init_ref.at[half], load_sem.at[4 + half])
        )
    for load in loads:
        load.start()

    barrier = pltpu.get_barrier_semaphore()
    for n, peer in ((n_inner, inner_id), (n_low, low_id), (n_high, high_id)):
        each(
            n,
            lambda k, peer=peer: pl.semaphore_signal(
                barrier, inc=1, device_id=peer(k), device_id_type=MESH
            ),
        )

    totals = dot(decay_ref[...], jnp.ones((length, send_total.shape[2]), BF16), NN)
    for e in range(n_inner):
        send_total[e] = totals[e * 2 * ratio : (e + 1) * 2 * ratio]

    pl.semaphore_wait(barrier, n_inner + n_low + n_high - 3)
    each(n_inner, lambda k: total_copy(k).start())
    total1[inner] = send_total[inner]

    def half_rows(half):
        return pl.ds(half * columns, columns)

    def group_slices(group):
        return (
            pl.ds(pl.multiple_of(group * columns, columns), columns),
            pl.ds(pl.multiple_of(group * depth, depth), depth),
        )

    def gain_of(half, k):
        to = inner_peer(k)
        wide, narrow = group_slices(2 * to + half)
        summed = spread_sums(decay_ref, 2 * to + half, ratio, width)
        weighted = x_ref[:, wide].astype(F32) * jnp.exp(summed[length - 1 :] - summed)
        return dot(weighted.astype(BF16), in_ref[:, narrow], TN).astype(BF16)

    def own_of(half, k):
        to = inner_peer(k)
        wide, narrow = group_slices(2 * to + half)
        summed = spread_sums(decay_ref, 2 * to + half, ratio, width)
        scaled = grad_ref[:, wide].astype(F32) * jnp.exp(summed)
        return dot(scaled.astype(BF16), out_ref[:, narrow], TN).astype(BF16)

    def send_gains(half):
        at = half_rows(half)

        def act(k):
            send_gain[inner_peer(k), at, :] = gain_of(half, k)
            inner_copy(1 + half, k, send_gain, gain1, at).start()

        each(n_inner, act)
        gain1[inner, at, :] = gain_of(half, 0)

    def fill_owns(half):
        at = half_rows(half)

        def act(k):
            send_own[inner_peer(k), at, :] = own_of(half, k)

        each(n_inner, act)
        own1[inner, at, :] = own_of(half, 0)

    def send_inner(stage, src, dst, half):
        each(n_inner, lambda k: inner_copy(stage + half, k, src, dst, half_rows(half)).start())

    def recv_inner(stage, src, dst, half):
        each(n_inner, lambda k: inner_copy(stage + half, k, src, dst, half_rows(half)).wait_recv())

    def sent_inner(stage, src, dst, half):
        each(n_inner, lambda k: inner_copy(stage + half, k, src, dst, half_rows(half)).wait_send())

    def keep_inner(src, dst, half):
        at = half_rows(half)
        dst[inner, at, :] = src[inner, at, :]

    def send_low(stage, src, dst, half):
        each(n_low, lambda k: low_copy(stage + half, k, src, dst, half).start())
        dst[half, low] = src[half, low]

    def recv_low(stage, src, dst, half):
        each(n_low, lambda k: low_copy(stage + half, k, src, dst, half).wait_recv())

    def sent_low(stage, src, dst, half):
        each(n_low, lambda k: low_copy(stage + half, k, src, dst, half).wait_send())

    def send_high(stage, src, dst, half):
        each(n_high, lambda k: high_copy(stage + half, k, src, dst, half).start())
        dst[half, high] = src[half]

    def recv_high(stage, src, dst, half):
        each(n_high, lambda k: high_copy(stage + half, k, src, dst, half).wait_recv())

    def sent_high(stage, src, dst, half):
        each(n_high, lambda k: high_copy(stage + half, k, src, dst, half).wait_send())

    def factor1(e, head):
        return jnp.exp(total1[e, pl.ds(head, 1), :])

    def factor2(e, half):
        return jnp.exp(total2[e, pl.ds(half * ratio + low, 1), :])

    def factor3(e, half):
        return jnp.exp(total3[e, pl.ds(half * ratio + low, 1), :])

    def head_rows(head):
        return pl.ds(pl.multiple_of(head * width, width), width)

    def fold_gains(half):
        def body(r, none):
            head = half * ratio + r
            at = head_rows(head)
            value = gain1[0, at, :].astype(F32)
            for e in range(1, n_inner):
                value = factor1(e, head) * value + gain1[e, at, :].astype(F32)
            send_gain2[half, r] = value.astype(BF16)
            return none

        lax.fori_loop(0, ratio, body, 0)

    def fold_owns(half):
        def body(r, none):
            head = half * ratio + r
            at = head_rows(head)
            value = own1[n_inner - 1, at, :].astype(F32)
            for e in range(n_inner - 2, -1, -1):
                value = factor1(e, head) * value + own1[e, at, :].astype(F32)
            send_own2[half, r] = value.astype(BF16)
            return none

        lax.fori_loop(0, ratio, body, 0)

    def fold_gains2(half):
        value = gain2[half, 0].astype(F32)
        for e in range(1, n_low):
            value = factor2(e, half) * value + gain2[half, e].astype(F32)
        send_gain3[half] = value.astype(BF16)

    def fold_owns2(half):
        value = own2[half, n_low - 1].astype(F32)
        for e in range(n_low - 2, -1, -1):
            value = factor2(e, half) * value + own2[half, e].astype(F32)
        send_own3[half] = value.astype(BF16)

    def spread_states(half):
        value = init_ref[half]
        for e in range(n_high - 1):
            later = factor3(e, half) * value + gain3[half, e].astype(F32)
            value = jnp.where(e < high, later, value)
        for e in range(n_low):
            send_before[half, e] = value.astype(BF16)
            if e < n_low - 1:
                value = factor2(e, half) * value + gain2[half, e].astype(F32)

    def spread_afters(half):
        value = jnp.zeros(init_ref.shape[1:], F32)
        first = value
        for e in range(n_high - 1, -1, -1):
            first = factor3(e, half) * first + own3[half, e].astype(F32)
            value = jnp.where(e > high, first, value)
        first = first.astype(BF16)
        for e in range(n_low - 1, -1, -1):
            send_behind[half, e, 0:width] = value.astype(BF16)
            send_behind[half, e, width:] = first
            if e > 0:
                value = factor2(e, half) * value + own2[half, e].astype(F32)

    def fill_states(half):
        def body(r, none):
            head = half * ratio + r
            at = head_rows(head)
            value = before[half, r].astype(F32)
            for e in range(n_inner):
                send_state[e, at, :] = value.astype(BF16)
                if e < n_inner - 1:
                    value = factor1(e, head) * value + gain1[e, at, :].astype(F32)
            return none

        lax.fori_loop(0, ratio, body, 0)
        keep_inner(send_state, state_ref, half)

    def fill_afters(half):
        def body(r, none):
            head = half * ratio + r
            at = head_rows(head)
            start_ref[at, :] = behind[half, r, width:]
            value = behind[half, r, 0:width].astype(F32)
            for e in range(n_inner - 1, -1, -1):
                send_after[e, at, :] = value.astype(BF16)
                if e > 0:
                    value = factor1(e, head) * value + own1[e, at, :].astype(F32)
            return none

        lax.fori_loop(0, ratio, body, 0)
        keep_inner(send_after, after_ref, half)

    gains, owns = (1, send_gain, gain1), (3, send_own, own1)
    states, afters = (5, send_state, state_ref), (7, send_after, after_ref)
    gains2, owns2 = (1, send_gain2, gain2), (3, send_own2, own2)
    befores, behinds = (5, send_before, before), (7, send_behind, behind)
    gains3, owns3 = (1, send_gain3, gain3), (3, send_own3, own3)

    loads[0].wait()
    loads[1].wait()
    send_gains(0)
    send_gains(1)

    each(n_inner, lambda k: total_copy(k).wait_recv())
    row = total1[0]
    for e in range(1, n_inner):
        row = row + total1[e]
    send_total2[...] = row
    each(n_low, lambda k: total2_copy(k).start())
    total2[low] = row

    loads[2].wait()
    loads[3].wait()
    fill_owns(0)
    fill_owns(1)

    each(n_low, lambda k: total2_copy(k).wait_recv())
    row = total2[0]
    for e in range(1, n_low):
        row = row + total2[e]
    send_total3[...] = row
    each(n_high, lambda k: total3_copy(k).start())
    total3[high] = row

    recv_inner(*gains, 0)
    fold_gains(0)
    send_low(*gains2, 0)
    sent_inner(*gains, 0)
    sent_inner(*gains, 1)
    send_inner(*owns, 0)
    recv_low(*gains2, 0)
    fold_gains2(0)
    send_high(*gains3, 0)
    each(n_high, lambda k: total3_copy(k).wait_recv())
    loads[4].wait()
    loads[5].wait()
    recv_inner(*gains, 1)
    fold_gains(1)
    send_low(*gains2, 1)
    recv_high(*gains3, 0)
    spread_states(0)
    send_low(*befores, 0)
    recv_low(*gains2, 1)
    fold_gains2(1)
    send_high(*gains3, 1)
    sent_inner(*owns, 0)
    send_inner(*owns, 1)
    recv_high(*gains3, 1)
    spread_states(1)
    send_low(*befores, 1)
    recv_inner(*owns, 0)
    fold_owns(0)
    send_low(*owns2, 0)
    recv_low(*befores, 0)
    fill_states(0)
    recv_low(*owns2, 0)
    fold_owns2(0)
    send_high(*owns3, 0)
    recv_low(*befores, 1)
    fill_states(1)
    sent_inner(*owns, 1)
    send_inner(*states, 0)
    recv_inner(*owns, 1)
    fold_owns(1)
    send_low(*owns2, 1)
    recv_high(*owns3, 0)
    spread_afters(0)
    send_low(*behinds, 0)
    recv_low(*owns2, 1)
    fold_owns2(1)
    send_high(*owns3, 1)
    sent_inner(*states, 0)
    send_inner(*states, 1)
    recv_high(*owns3, 1)
    spread_afters(1)
    send_low(*behinds, 1)
    recv_low(*behinds, 0)
    fill_afters(0)
    sent_inner(*states, 1)
    send_inner(*afters, 0)
    recv_low(*behinds, 1)
    fill_afters(1)
    sent_inner(*afters, 0)
    send_inner(*afters, 1)

    each(n_inner, lambda k: total_copy(k).wait_send())
    each(n_low, lambda k: total2_copy(k).wait_send())
    each(n_high, lambda k: total3_copy(k).wait_send())
    for half in range(2):
        for stage in (gains2, owns2, befores, behinds):
            sent_low(*stage, half)
        for stage in (gains3, owns3):
            sent_high(*stage, half)
        recv_inner(*states, half)
    recv_inner(*afters, 0)
    recv_inner(*afters, 1)
    sent_inner(*afters, 1)


def carry(x, decay, read_in, read_out, grad, init, n_outer, n_inner, width, depth):
    length = x.shape[0]
    groups = read_in.shape[1] // depth
    heads = decay.shape[0]
    ratio = heads // groups
    mine = heads // n_inner
    n_low = ratio
    n_high = n_outer // n_low
    vmem = pl.BlockSpec(memory_space=pltpu.VMEM)
    hbm = pl.BlockSpec(memory_space=pl.ANY)
    chunks = pltpu.VMEM((n_inner, mine * width, depth), BF16)
    runs = pltpu.VMEM((2, n_low, width, depth), BF16)
    doubles = pltpu.VMEM((2, n_low, 2 * width, depth), BF16)
    head = pltpu.VMEM((2, width, depth), BF16)
    highs = pltpu.VMEM((2, n_high, width, depth), BF16)
    total = pltpu.VMEM((mine, depth), F32)
    state = jax.ShapeDtypeStruct((n_inner, mine * width, depth), BF16)
    dma = pltpu.SemaphoreType.DMA
    return pl.pallas_call(
        functools.partial(carry_kernel, n_inner, n_low, n_high, ratio, width),
        in_specs=[hbm, vmem, hbm, hbm, hbm, hbm],
        out_specs=[vmem] * 3,
        out_shape=[state, state, jax.ShapeDtypeStruct((mine * width, depth), BF16)],
        scratch_shapes=[
            pltpu.VMEM(x.shape, BF16),
            pltpu.VMEM(read_in.shape, BF16),
            pltpu.VMEM(read_out.shape, BF16),
            pltpu.VMEM(grad.shape, BF16),
            pltpu.VMEM((2, width, depth), F32),
            pltpu.VMEM((n_inner, mine, depth), F32),
            pltpu.VMEM((n_inner, mine, depth), F32),
            total,
            pltpu.VMEM((n_low, mine, depth), F32),
            total,
            pltpu.VMEM((n_high, mine, depth), F32),
            chunks,
            chunks,
            chunks,
            chunks,
            runs,
            runs,
            runs,
            runs,
            head,
            highs,
            head,
            highs,
            runs,
            runs,
            doubles,
            doubles,
            chunks,
            chunks,
            dma((6,)),
            dma((9, n_inner)),
            dma((9, n_inner)),
            dma((9, n_low)),
            dma((9, n_low)),
            dma((5, n_high)),
            dma((5, n_high)),
        ],
        compiler_params=pltpu.CompilerParams(
            collective_id=0, has_side_effects=True, vmem_limit_bytes=48 * 2**20
        ),
        name="carry",
    )(x, decay, read_in, read_out, grad, init)


def block_kernel(
    ratio,
    width,
    x_ref,
    decay_ref,
    in_ref,
    out_ref,
    grad_ref,
    state_ref,
    after_ref,
    start_ref,
    y_ref,
    dx_ref,
    ddecay_ref,
    din_ref,
    dout_ref,
    dstart_ref,
    upper_sum,
    lower_sum,
    state_sum,
):
    group = pl.program_id(0)
    length = x_ref.shape[0]
    heads = decay_ref.shape[0]
    columns = ratio * width
    dstart_ref[...] = start_ref[...].astype(F32)

    summed = spread_sums(decay_ref, group, ratio, width)
    from_start = jnp.exp(summed)
    to_end = jnp.exp(summed[length - 1 :] - summed)
    picked = head_decays(decay_ref, group, ratio)
    low = lower(length)
    down = dot(low, picked, NT)
    across = dot(picked, low, NT)
    x = x_ref[...]
    grad = grad_ref[...]
    x32 = x.astype(F32)
    grad32 = grad.astype(F32)
    b = in_ref[...]
    c = out_ref[...]
    state = state_ref[...]
    after = after_ref[...]
    scores = dot(c, b, NT)
    causal = iota((length, length), 0) >= iota((length, length), 1)

    local = []
    local_dx = []
    dscores = jnp.zeros((length, length), F32)
    for r in range(ratio):
        gap = down[:, r : r + 1] - across[r : r + 1, :]
        decays = jnp.exp(jnp.where(causal, gap, -1e30))
        weights = (scores * decays).astype(BF16)
        at = slice(r * width, (r + 1) * width)
        local.append(dot(weights, x[:, at], NN))
        local_dx.append(dot(weights, grad[:, at], TN))
        dscores = dscores + dot(grad[:, at], x[:, at], NT) * decays
    y = jnp.concatenate(local, axis=1) + dot(c, state, NT) * from_start
    y_ref[...] = y.astype(BF16)
    near_dx = jnp.concatenate(local_dx, axis=1)
    far_dx = dot(b, after, NT) * to_end
    dx_ref[...] = (near_dx + far_dx).astype(BF16)

    dscores = dscores.astype(BF16)
    dout_ref[...] = (
        dot(dscores, b, NN) + dot((grad32 * from_start).astype(BF16), state, NN)
    ).astype(BF16)
    din_ref[...] = (dot(dscores, c, TN) + dot((x32 * to_end).astype(BF16), after, NN)).astype(BF16)

    place = as_bf16(iota((columns, heads), 1) == group * ratio + iota((columns, heads), 0) // width)
    up = split_dot(y * grad32 - x32 * near_dx, place, NN)
    lo = split_dot(x32 * far_dx, place, NN)
    product = state.astype(F32) * after.astype(F32)
    total = dot(picked, jnp.ones((length, product.shape[1]), BF16), NN)
    state_sum[pl.ds(pl.multiple_of(group * ratio, ratio), ratio), :] = (
        jnp.sum(product.reshape(ratio, width, product.shape[1]), axis=1) * jnp.exp(total)
    )

    @pl.when(group == 0)
    def _():
        upper_sum[...] = up
        lower_sum[...] = lo

    @pl.when(group > 0)
    def _():
        upper_sum[...] += up
        lower_sum[...] += lo

    @pl.when(group == pl.num_programs(0) - 1)
    def _():
        row = iota((length, length), 0)
        column = iota((length, length), 1)
        up_mask = jnp.where(row >= column, 1.0, 0.0)
        low_mask = jnp.where(row < column, 1.0, 0.0)
        ddecay_ref[...] = (
            exact_dot(upper_sum[...], up_mask, TN)
            + exact_dot(lower_sum[...], low_mask, TN)
            + jnp.sum(state_sum[...], axis=1, keepdims=True)
        ).astype(BF16)


def block(x, decay, read_in, read_out, grad, state, after, start, heads, width, depth):
    length = x.shape[0]
    groups = read_in.shape[1] // depth
    ratio = heads // groups
    columns = ratio * width
    share = start.shape[0] // groups
    wide = pl.BlockSpec((length, columns), lambda g: (0, g))
    narrow = pl.BlockSpec((length, depth), lambda g: (0, g))
    tall = pl.BlockSpec((columns, depth), lambda g: (g, 0))
    part = pl.BlockSpec((share, depth), lambda g: (g, 0))
    whole = pl.BlockSpec((heads, length), lambda g: (0, 0))
    return pl.pallas_call(
        functools.partial(block_kernel, ratio, width),
        grid=(groups,),
        in_specs=[wide, whole, narrow, narrow, wide, tall, tall, part],
        out_specs=[wide, wide, whole, narrow, narrow, part],
        out_shape=[
            jax.ShapeDtypeStruct(x.shape, BF16),
            jax.ShapeDtypeStruct(x.shape, BF16),
            jax.ShapeDtypeStruct(decay.shape, BF16),
            jax.ShapeDtypeStruct(read_in.shape, BF16),
            jax.ShapeDtypeStruct(read_out.shape, BF16),
            jax.ShapeDtypeStruct(start.shape, F32),
        ],
        scratch_shapes=[
            pltpu.VMEM((length, heads), F32),
            pltpu.VMEM((length, heads), F32),
            pltpu.VMEM((heads, depth), F32),
        ],
        name="block",
    )(x, decay, read_in, read_out, grad, state, after, start)


def shards(inputs, log_decay, read_in, read_out, initial_state, output_grad):
    n_outer, n_inner = lax.axis_size("outer"), lax.axis_size("inner")
    own_heads, width, depth = initial_state.shape
    heads = own_heads * n_inner
    decay = log_decay.T
    tokens = (inputs, decay, read_in, read_out, output_grad)
    state, after, start = carry(
        *tokens, initial_state.reshape(-1, depth), n_outer, n_inner, width, depth
    )
    y, dx, ddecay, din, dout, dstart = block(
        *tokens,
        state.reshape(-1, depth),
        after.reshape(-1, depth),
        start,
        heads,
        width,
        depth,
    )
    return (y, dx, ddecay.T, din, dout, dstart.reshape(initial_state.shape))


def solution(mesh):
    tokens = P(("outer", "inner"), None)
    held = P("inner", None, None)
    return jax.shard_map(
        shards,
        mesh=mesh,
        in_specs=(tokens, tokens, tokens, tokens, held, tokens),
        out_specs=(tokens, tokens, tokens, tokens, tokens, held),
        check_vma=False,
    )
```

time: 102 us -> 88.6 us (0.87); the launches traced: 100 us -> 88.2 us
  Pallas kernels: 90.9 us -> 78.7 us
    pallas_call x2 -> x1, Pallas kernels: 75.1 us -> 62.7 us  [carry(): pl.pallas_call(functools.partial(carry_kernel, n_inner, n_low, n_high, ra...]
    unnamed x16 -> x18, local copies, waits for them, and re-layouts: 8.75 us -> 8.79 us
where the time goes in v2:
time: 88.6 us; the launch traced here: 88.2 us
  Pallas kernels  78.7 us (89%)
  local copies, waits for them, and re-layouts  8.79 us (10%)
    pallas_call x1, Pallas kernels, carry(): pl.pallas_call(functools.partial(carry_kernel, n_inner, n_low, n_high, ra...  62.7 us
    pallas_call x1, Pallas kernels, block(): pl.pallas_call(functools.partial(block_kernel, ratio, width), grid=(group...  16 us
    unnamed x18, local copies, waits for them, and re-layouts  8.79 us

profile of v2, /device:TPU:0, one launch (start us, length us, event | category | flops | bytes accessed | tf_op | source)
XLA Modules:
  0.0 88.2 jit_solution(7736237222575770274)
XLA Ops:
  0.6 0.0 copy-start
  0.6 1.2 %copy-done = bf16[128,4096]{1,0:T(8,128)(2,1)S(1)} copy-done((bf16[128,4096]{1,0:T(8,128)(2,1)S(1)}, bf16[128,4096]{1,0:T(8,128)(2,1)}, u32[]{:S(2)}) %copy-start) | copy-done | bytes 1048600
  1.9 0.0 copy-start.1
  1.9 1.2 %copy-done.1 = bf16[128,4096]{1,0:T(8,128)(2,1)S(1)} copy-done((bf16[128,4096]{1,0:T(8,128)(2,1)S(1)}, bf16[128,4096]{1,0:T(8,128)(2,1)}, u32[]{:S(2)}) %copy-start.1) | copy-done | bytes 1048600
  3.1 0.0 copy-start.4
  3.1 0.9 %copy-done.4 = bf16[128,1024]{1,0:T(8,128)(2,1)S(1)} copy-done((bf16[128,1024]{1,0:T(8,128)(2,1)S(1)}, bf16[128,1024]{1,0:T(8,128)(2,1)}, u32[]{:S(2)}) %copy-start.4) | copy-done | bytes 262168
  4.0 0.0 copy-start.5
  4.0 0.9 %copy-done.5 = bf16[128,1024]{1,0:T(8,128)(2,1)S(1)} copy-done((bf16[128,1024]{1,0:T(8,128)(2,1)S(1)}, bf16[128,1024]{1,0:T(8,128)(2,1)}, u32[]{:S(2)}) %copy-start.5) | copy-done | bytes 262168
  5.0 0.0 copy-start.6
  5.0 1.0 %copy-done.6 = f32[16,64,128]{2,1,0:T(8,128)S(1)} copy-done((f32[16,64,128]{2,1,0:T(8,128)S(1)}, f32[16,64,128]{2,1,0:T(8,128)}, u32[]{:S(2)}) %copy-start.6) | copy-done | bytes 524312
  6.0 0.0 copy-start.8
  6.0 0.7 copy-done.8
  6.7 62.7 %carry.1 = (bf16[4,1024,128]{2,1,0:T(8,128)(2,1)S(1)}, bf16[4,1024,128]{2,1,0:T(8,128)(2,1)S(1)}, bf16[1024,128]{1,0:T(8,128)(2,1)S(1)}) custom-call(bf16[128,4096]{1,0:T(8,128)(2,1)S(1)} %copy-done, bf16[64,128]{1,0:T(8,128)(2,1)S(1)} %bitcast.10, bf16[128,1024]{1,0:T(8,128)(2,1)S(1)} %copy-done.4, bf16[128,1024]{1,0:T(8,128)(2,1)S(1)} %copy-done.5, ...), custom_call_target="tpu_custom_call" | custom-call | tf_op jit(solution)/shard_map/carry/pallas_call | solution.py:531
  69.5 0.0 copy-start.2
  69.5 1.0 %copy-done.2 = bf16[4,1024,128]{2,1,0:T(8,128)(2,1)} copy-done((bf16[4,1024,128]{2,1,0:T(8,128)(2,1)}, bf16[4,1024,128]{2,1,0:T(8,128)(2,1)S(1)}, u32[]{:S(2)}) %copy-start.2) | copy-done | bytes 1048600
  70.4 0.0 copy-start.3
  70.4 1.0 %copy-done.3 = bf16[4,1024,128]{2,1,0:T(8,128)(2,1)} copy-done((bf16[4,1024,128]{2,1,0:T(8,128)(2,1)}, bf16[4,1024,128]{2,1,0:T(8,128)(2,1)S(1)}, u32[]{:S(2)}) %copy-start.3) | copy-done | bytes 1048600
  71.5 0.0 copy-start.7
  71.5 0.7 copy-done.7
  72.2 16.0 %block.1 = (bf16[128,4096]{1,0:T(8,128)(2,1)}, bf16[128,4096]{1,0:T(8,128)(2,1)}, bf16[64,128]{1,0:T(8,128)(2,1)}, bf16[128,1024]{1,0:T(8,128)(2,1)}, bf16[128,1024]{1,0:T(8,128)(2,1)}, /*index=5*/f32[1024,128]{1,0:T(8,128)}) custom-call(bf16[128,4096]{1,0:T(8,128)(2,1)} %x_ref.1, bf16[64,128]{1,0:T(8,128)(2,1)} %bitcast.9, bf16[128,1024]{1,0:T(8,128)(2,1)} %in_ref.1, ...), custom_call_target="tpu_custom_call" | custom-call | tf_op jit(solution)/shard_map/block/pallas_call | solution.py:692
Async XLA Ops:
  0.6 1.2 %copy-start = (bf16[128,4096]{1,0:T(8,128)(2,1)S(1)}, bf16[128,4096]{1,0:T(8,128)(2,1)}, u32[]{:S(2)}) copy-start(bf16[128,4096]{1,0:T(8,128)(2,1)} %x_ref.1) | copy-start | bytes 3145732
  1.9 1.2 %copy-start.1 = (bf16[128,4096]{1,0:T(8,128)(2,1)S(1)}, bf16[128,4096]{1,0:T(8,128)(2,1)}, u32[]{:S(2)}) copy-start(bf16[128,4096]{1,0:T(8,128)(2,1)} %grad_ref.1) | copy-start | bytes 3145732
  3.1 0.9 %copy-start.4 = (bf16[128,1024]{1,0:T(8,128)(2,1)S(1)}, bf16[128,1024]{1,0:T(8,128)(2,1)}, u32[]{:S(2)}) copy-start(bf16[128,1024]{1,0:T(8,128)(2,1)} %in_ref.1) | copy-start | bytes 786436
  4.0 0.9 %copy-start.5 = (bf16[128,1024]{1,0:T(8,128)(2,1)S(1)}, bf16[128,1024]{1,0:T(8,128)(2,1)}, u32[]{:S(2)}) copy-start(bf16[128,1024]{1,0:T(8,128)(2,1)} %out_ref.1) | copy-start | bytes 786436
  5.0 1.0 %copy-start.6 = (f32[16,64,128]{2,1,0:T(8,128)S(1)}, f32[16,64,128]{2,1,0:T(8,128)}, u32[]{:S(2)}) copy-start(f32[16,64,128]{2,1,0:T(8,128)} %param.10) | copy-start | bytes 1572868
  6.0 0.7 copy-start.8
  69.5 1.0 %copy-start.2 = (bf16[4,1024,128]{2,1,0:T(8,128)(2,1)}, bf16[4,1024,128]{2,1,0:T(8,128)(2,1)S(1)}, u32[]{:S(2)}) copy-start(bf16[4,1024,128]{2,1,0:T(8,128)(2,1)S(1)} %get-tuple-element.15) | copy-start | bytes 3145732
  70.4 1.0 %copy-start.3 = (bf16[4,1024,128]{2,1,0:T(8,128)(2,1)}, bf16[4,1024,128]{2,1,0:T(8,128)(2,1)S(1)}, u32[]{:S(2)}) copy-start(bf16[4,1024,128]{2,1,0:T(8,128)(2,1)S(1)} %get-tuple-element.16) | copy-start | bytes 3145732
  71.5 0.7 copy-start.7

commit v3 on v2

--- a/solution.py
+++ b/solution.py
@@ -68,9 +68,31 @@
     out_hbm,
     grad_hbm,
     init_hbm,
+    y_hbm,
+    dx_hbm,
+    ddecay_hbm,
+    din_hbm,
+    dout_hbm,
+    dstart_hbm,
     state_ref,
     after_ref,
     start_ref,
+    from_start,
+    to_end,
+    weighted_ref,
+    scaled_ref,
+    y_sum,
+    dx_sum,
+    din_sum,
+    dout_sum,
+    up_sum,
+    low_sum,
+    state_sum,
+    y_ref,
+    dx_ref,
+    ddecay_ref,
+    din_ref,
+    dout_ref,
     x_ref,
     in_ref,
     out_ref,
@@ -101,6 +123,7 @@
     send_state,
     send_after,
     load_sem,
+    store_sem,
     inner_send,
     inner_recv,
     low_send,
@@ -238,18 +261,102 @@
         )
 
     def gain_of(half, k):
-        to = inner_peer(k)
-        wide, narrow = group_slices(2 * to + half)
-        summed = spread_sums(decay_ref, 2 * to + half, ratio, width)
-        weighted = x_ref[:, wide].astype(F32) * jnp.exp(summed[length - 1 :] - summed)
-        return dot(weighted.astype(BF16), in_ref[:, narrow], TN).astype(BF16)
+        group = 2 * inner_peer(k) + half
+        wide, narrow = group_slices(group)
+        summed = spread_sums(decay_ref, group, ratio, width)
+        from_start[:, wide] = jnp.exp(summed)
+        factor = jnp.exp(summed[length - 1 :] - summed)
+        to_end[:, wide] = factor
+        weighted = (x_ref[:, wide].astype(F32) * factor).astype(BF16)
+        weighted_ref[:, wide] = weighted
+        return dot(weighted, in_ref[:, narrow], TN).astype(BF16)
 
     def own_of(half, k):
-        to = inner_peer(k)
-        wide, narrow = group_slices(2 * to + half)
-        summed = spread_sums(decay_ref, 2 * to + half, ratio, width)
-        scaled = grad_ref[:, wide].astype(F32) * jnp.exp(summed)
-        return dot(scaled.astype(BF16), out_ref[:, narrow], TN).astype(BF16)
+        wide, narrow = group_slices(2 * inner_peer(k) + half)
+        scaled = (grad_ref[:, wide].astype(F32) * from_start[:, wide]).astype(BF16)
+        scaled_ref[:, wide] = scaled
+        return dot(scaled, out_ref[:, narrow], TN).astype(BF16)
+
+    def local_part(group):
+        wide, narrow = group_slices(group)
+        picked = head_decays(decay_ref, group, ratio)
+        below = lower(length)
+        down = dot(below, picked, NT)
+        across = dot(picked, below, NT)
+        x, grad = x_ref[:, wide], grad_ref[:, wide]
+        b, c = in_ref[:, narrow], out_ref[:, narrow]
+        scores = dot(c, b, NT)
+        causal = iota((length, length), 0) >= iota((length, length), 1)
+        ys, dxs = [], []
+        dscores = jnp.zeros((length, length), F32)
+        for r in range(ratio):
+            gap = down[:, r : r + 1] - across[r : r + 1, :]
+            decays = jnp.exp(jnp.where(causal, gap, -1e30))
+            weights = (scores * decays).astype(BF16)
+            at = slice(r * width, (r + 1) * width)
+            ys.append(dot(weights, x[:, at], NN))
+            dxs.append(dot(weights, grad[:, at], TN))
+            dscores = dscores + dot(grad[:, at], x[:, at], NT) * decays
+        y_sum[:, wide] = jnp.concatenate(ys, axis=1)
+        dx_sum[:, wide] = jnp.concatenate(dxs, axis=1)
+        dscores = dscores.astype(BF16)
+        dout_sum[:, narrow] = dot(dscores, b, NN)
+        din_sum[:, narrow] = dot(dscores, c, TN)
+
+    def place(group):
+        heads = decay_ref.shape[0]
+        head = group * ratio + iota((columns, heads), 0) // width
+        return as_bf16(iota((columns, heads), 1) == head)
+
+    def state_part(half, k):
+        owner = inner_peer(n_inner - k)
+        group = 2 * owner + half
+        wide, narrow = group_slices(group)
+        state = state_ref[owner, half_rows(half), :]
+        y = y_sum[:, wide] + dot(out_ref[:, narrow], state, NT) * from_start[:, wide]
+        y_ref[:, wide] = y.astype(BF16)
+        dout = dout_sum[:, narrow] + dot(scaled_ref[:, wide], state, NN)
+        dout_ref[:, narrow] = dout.astype(BF16)
+        change = y * grad_ref[:, wide].astype(F32) - x_ref[:, wide].astype(F32) * dx_sum[:, wide]
+        up_sum[...] += split_dot(change, place(group), NN)
+
+    def after_part(half, k):
+        owner = inner_peer(n_inner - k)
+        group = 2 * owner + half
+        wide, narrow = group_slices(group)
+        state = state_ref[owner, half_rows(half), :]
+        after = after_ref[owner, half_rows(half), :]
+        far = dot(in_ref[:, narrow], after, NT) * to_end[:, wide]
+        dx_ref[:, wide] = (dx_sum[:, wide] + far).astype(BF16)
+        din = din_sum[:, narrow] + dot(weighted_ref[:, wide], after, NN)
+        din_ref[:, narrow] = din.astype(BF16)
+        low_sum[...] += split_dot(x_ref[:, wide].astype(F32) * far, place(group), NN)
+        product = state.astype(F32) * after.astype(F32)
+        picked = head_decays(decay_ref, group, ratio)
+        total = dot(picked, jnp.ones((length, depth), BF16), NN)
+        state_sum[pl.ds(pl.multiple_of(group * ratio, ratio), ratio), :] = jnp.sum(
+            product.reshape(ratio, width, depth), axis=1
+        ) * jnp.exp(total)
+
+    def local_parts(start, stop):
+        def body(group, none):
+            local_part(group)
+            return none
+
+        groups = n_inner * 2
+        lax.fori_loop(start * groups // 8, stop * groups // 8, body, 0)
+
+    def parts(stage, half, part):
+        part(half, 0)
+
+        def act(k):
+            inner_copy(stage[0] + half, k, stage[1], stage[2], half_rows(half)).wait_recv()
+            part(half, k)
+
+        each(n_inner, act)
+
+    def store(i, src, dst):
+        return pltpu.make_async_copy(src, dst, store_sem.at[i])
 
     def send_gains(half):
         at = half_rows(half)
@@ -392,7 +499,7 @@
         def body(r, none):
             head = half * ratio + r
             at = head_rows(head)
-            start_ref[at, :] = behind[half, r, width:]
+            start_ref[at, :] = behind[half, r, width:].astype(F32)
             value = behind[half, r, 0:width].astype(F32)
             for e in range(n_inner - 1, -1, -1):
                 send_after[e, at, :] = value.astype(BF16)
@@ -435,15 +542,19 @@
     each(n_high, lambda k: total3_copy(k).start())
     total3[high] = row
 
+    up_sum[...] = jnp.zeros_like(up_sum)
+    low_sum[...] = jnp.zeros_like(low_sum)
+
     recv_inner(*gains, 0)
     fold_gains(0)
     send_low(*gains2, 0)
+    local_parts(0, 1)
+    recv_low(*gains2, 0)
+    fold_gains2(0)
+    send_high(*gains3, 0)
     sent_inner(*gains, 0)
     sent_inner(*gains, 1)
     send_inner(*owns, 0)
-    recv_low(*gains2, 0)
-    fold_gains2(0)
-    send_high(*gains3, 0)
     each(n_high, lambda k: total3_copy(k).wait_recv())
     loads[4].wait()
     loads[5].wait()
@@ -453,6 +564,7 @@
     recv_high(*gains3, 0)
     spread_states(0)
     send_low(*befores, 0)
+    local_parts(1, 2)
     recv_low(*gains2, 1)
     fold_gains2(1)
     send_high(*gains3, 1)
@@ -479,6 +591,7 @@
     recv_high(*owns3, 0)
     spread_afters(0)
     send_low(*behinds, 0)
+    local_parts(2, 3)
     recv_low(*owns2, 1)
     fold_owns2(1)
     send_high(*owns3, 1)
@@ -489,12 +602,21 @@
     send_low(*behinds, 1)
     recv_low(*behinds, 0)
     fill_afters(0)
+    local_parts(3, 6)
     sent_inner(*states, 1)
     send_inner(*afters, 0)
     recv_low(*behinds, 1)
     fill_afters(1)
+    store_start = store(0, start_ref, dstart_hbm)
+    store_start.start()
+    local_parts(6, 8)
+    parts(states, 0, state_part)
     sent_inner(*afters, 0)
     send_inner(*afters, 1)
+    parts(states, 1, state_part)
+    stores = [store(1, y_ref, y_hbm), store(2, dout_ref, dout_hbm)]
+    for copy in stores:
+        copy.start()
 
     each(n_inner, lambda k: total_copy(k).wait_send())
     each(n_low, lambda k: total2_copy(k).wait_send())
@@ -504,10 +626,22 @@
             sent_low(*stage, half)
         for stage in (gains3, owns3):
             sent_high(*stage, half)
-        recv_inner(*states, half)
-    recv_inner(*afters, 0)
-    recv_inner(*afters, 1)
+    parts(afters, 0, after_part)
     sent_inner(*afters, 1)
+    parts(afters, 1, after_part)
+
+    row = iota((length, length), 0)
+    column = iota((length, length), 1)
+    ddecay_ref[...] = (
+        exact_dot(up_sum[...], jnp.where(row >= column, 1.0, 0.0), TN)
+        + exact_dot(low_sum[...], jnp.where(row < column, 1.0, 0.0), TN)
+        + jnp.sum(state_sum[...], axis=1, keepdims=True)
+    ).astype(BF16)
+    ends = [store(3, dx_ref, dx_hbm), store(4, din_ref, din_hbm), store(5, ddecay_ref, ddecay_hbm)]
+    for copy in ends:
+        copy.start()
+    for copy in [store_start] + stores + ends:
+        copy.wait()
 
 
 def carry(x, decay, read_in, read_out, grad, init, n_outer, n_inner, width, depth):
@@ -526,14 +660,43 @@
     head = pltpu.VMEM((2, width, depth), BF16)
     highs = pltpu.VMEM((2, n_high, width, depth), BF16)
     total = pltpu.VMEM((mine, depth), F32)
-    state = jax.ShapeDtypeStruct((n_inner, mine * width, depth), BF16)
+    wide = jax.ShapeDtypeStruct(x.shape, BF16)
+    narrow = jax.ShapeDtypeStruct(read_in.shape, BF16)
+    wide32 = pltpu.VMEM(x.shape, F32)
+    narrow32 = pltpu.VMEM(read_in.shape, F32)
     dma = pltpu.SemaphoreType.DMA
     return pl.pallas_call(
         functools.partial(carry_kernel, n_inner, n_low, n_high, ratio, width),
         in_specs=[hbm, vmem, hbm, hbm, hbm, hbm],
-        out_specs=[vmem] * 3,
-        out_shape=[state, state, jax.ShapeDtypeStruct((mine * width, depth), BF16)],
+        out_specs=[hbm] * 6,
+        out_shape=[
+            wide,
+            wide,
+            jax.ShapeDtypeStruct(decay.shape, BF16),
+            narrow,
+            narrow,
+            jax.ShapeDtypeStruct((mine * width, depth), F32),
+        ],
         scratch_shapes=[
+            chunks,
+            chunks,
+            pltpu.VMEM((mine * width, depth), F32),
+            wide32,
+            wide32,
+            pltpu.VMEM(x.shape, BF16),
+            pltpu.VMEM(x.shape, BF16),
+            wide32,
+            wide32,
+            narrow32,
+            narrow32,
+            pltpu.VMEM((length, heads), F32),
+            pltpu.VMEM((length, heads), F32),
+            pltpu.VMEM((heads, depth), F32),
+            pltpu.VMEM(x.shape, BF16),
+            pltpu.VMEM(x.shape, BF16),
+            pltpu.VMEM(decay.shape, BF16),
+            pltpu.VMEM(read_in.shape, BF16),
+            pltpu.VMEM(read_out.shape, BF16),
             pltpu.VMEM(x.shape, BF16),
             pltpu.VMEM(read_in.shape, BF16),
             pltpu.VMEM(read_out.shape, BF16),
@@ -564,6 +727,7 @@
             chunks,
             chunks,
             dma((6,)),
+            dma((6,)),
             dma((9, n_inner)),
             dma((9, n_inner)),
             dma((9, n_low)),
@@ -572,163 +736,58 @@
             dma((5, n_high)),
         ],
         compiler_params=pltpu.CompilerParams(
-            collective_id=0, has_side_effects=True, vmem_limit_bytes=48 * 2**20
+            collective_id=0, has_side_effects=True, vmem_limit_bytes=60 * 2**20
         ),
         name="carry",
     )(x, decay, read_in, read_out, grad, init)
 
 
-def block_kernel(
-    ratio,
-    width,
-    x_ref,
-    decay_ref,
-    in_ref,
-    out_ref,
-    grad_ref,
-    state_ref,
-    after_ref,
-    start_ref,
-    y_ref,
-    dx_ref,
-    ddecay_ref,
-    din_ref,
-    dout_ref,
-    dstart_ref,
-    upper_sum,
-    lower_sum,
-    state_sum,
-):
-    group = pl.program_id(0)
-    length = x_ref.shape[0]
-    heads = decay_ref.shape[0]
-    columns = ratio * width
-    dstart_ref[...] = start_ref[...].astype(F32)
-
-    summed = spread_sums(decay_ref, group, ratio, width)
-    from_start = jnp.exp(summed)
-    to_end = jnp.exp(summed[length - 1 :] - summed)
-    picked = head_decays(decay_ref, group, ratio)
-    low = lower(length)
-    down = dot(low, picked, NT)
-    across = dot(picked, low, NT)
-    x = x_ref[...]
-    grad = grad_ref[...]
-    x32 = x.astype(F32)
-    grad32 = grad.astype(F32)
-    b = in_ref[...]
-    c = out_ref[...]
-    state = state_ref[...]
-    after = after_ref[...]
-    scores = dot(c, b, NT)
-    causal = iota((length, length), 0) >= iota((length, length), 1)
-
-    local = []
-    local_dx = []
-    dscores = jnp.zeros((length, length), F32)
-    for r in range(ratio):
-        gap = down[:, r : r + 1] - across[r : r + 1, :]
-        decays = jnp.exp(jnp.where(causal, gap, -1e30))
-        weights = (scores * decays).astype(BF16)
-        at = slice(r * width, (r + 1) * width)
-        local.append(dot(weights, x[:, at], NN))
-        local_dx.append(dot(weights, grad[:, at], TN))
-        dscores = dscores + dot(grad[:, at], x[:, at], NT) * decays
-    y = jnp.concatenate(local, axis=1) + dot(c, state, NT) * from_start
-    y_ref[...] = y.astype(BF16)
-    near_dx = jnp.concatenate(local_dx, axis=1)
-    far_dx = dot(b, after, NT) * to_end
-    dx_ref[...] = (near_dx + far_dx).astype(BF16)
-
-    dscores = dscores.astype(BF16)
-    dout_ref[...] = (
-        dot(dscores, b, NN) + dot((grad32 * from_start).astype(BF16), state, NN)
-    ).astype(BF16)
-    din_ref[...] = (dot(dscores, c, TN) + dot((x32 * to_end).astype(BF16), after, NN)).astype(BF16)
-
-    place = as_bf16(iota((columns, heads), 1) == group * ratio + iota((columns, heads), 0) // width)
-    up = split_dot(y * grad32 - x32 * near_dx, place, NN)
-    lo = split_dot(x32 * far_dx, place, NN)
-    product = state.astype(F32) * after.astype(F32)
-    total = dot(picked, jnp.ones((length, product.shape[1]), BF16), NN)
-    state_sum[pl.ds(pl.multiple_of(group * ratio, ratio), ratio), :] = (
-        jnp.sum(product.reshape(ratio, width, product.shape[1]), axis=1) * jnp.exp(total)
-    )
-
-    @pl.when(group == 0)
-    def _():
-        upper_sum[...] = up
-        lower_sum[...] = lo
-
-    @pl.when(group > 0)
-    def _():
-        upper_sum[...] += up
-        lower_sum[...] += lo
-
-    @pl.when(group == pl.num_programs(0) - 1)
-    def _():
-        row = iota((length, length), 0)
-        column = iota((length, length), 1)
-        up_mask = jnp.where(row >= column, 1.0, 0.0)
-        low_mask = jnp.where(row < column, 1.0, 0.0)
-        ddecay_ref[...] = (
-            exact_dot(upper_sum[...], up_mask, TN)
-            + exact_dot(lower_sum[...], low_mask, TN)
-            + jnp.sum(state_sum[...], axis=1, keepdims=True)
-        ).astype(BF16)
-
-
-def block(x, decay, read_in, read_out, grad, state, after, start, heads, width, depth):
-    length = x.shape[0]
-    groups = read_in.shape[1] // depth
-    ratio = heads // groups
-    columns = ratio * width
-    share = start.shape[0] // groups
-    wide = pl.BlockSpec((length, columns), lambda g: (0, g))
-    narrow = pl.BlockSpec((length, depth), lambda g: (0, g))
-    tall = pl.BlockSpec((columns, depth), lambda g: (g, 0))
-    part = pl.BlockSpec((share, depth), lambda g: (g, 0))
-    whole = pl.BlockSpec((heads, length), lambda g: (0, 0))
+def deliver_kernel(*refs):
+    n = (len(refs) - 2) // 3
+    hbm, out, held, (loaded, stored) = refs[:n], refs[n : 2 * n], refs[2 * n : 3 * n], refs[3 * n :]
+    loads = [pltpu.make_async_copy(hbm[i], held[i], loaded.at[i]) for i in range(n)]
+    stores = [pltpu.make_async_copy(held[i], out[i], stored.at[i]) for i in range(n)]
+    for load in loads:
+        load.start()
+    for load, store in zip(loads, stores):
+        load.wait()
+        store.start()
+    for store in stores:
+        store.wait()
+
+
+def deliver(*arrays):
+    n = len(arrays)
+    hbm = pl.BlockSpec(memory_space=pl.ANY)
     return pl.pallas_call(
-        functools.partial(block_kernel, ratio, width),
-        grid=(groups,),
-        in_specs=[wide, whole, narrow, narrow, wide, tall, tall, part],
-        out_specs=[wide, wide, whole, narrow, narrow, part],
-        out_shape=[
-            jax.ShapeDtypeStruct(x.shape, BF16),
-            jax.ShapeDtypeStruct(x.shape, BF16),
-            jax.ShapeDtypeStruct(decay.shape, BF16),
-            jax.ShapeDtypeStruct(read_in.shape, BF16),
-            jax.ShapeDtypeStruct(read_out.shape, BF16),
-            jax.ShapeDtypeStruct(start.shape, F32),
-        ],
-        scratch_shapes=[
-            pltpu.VMEM((length, heads), F32),
-            pltpu.VMEM((length, heads), F32),
-            pltpu.VMEM((heads, depth), F32),
-        ],
-        name="block",
-    )(x, decay, read_in, read_out, grad, state, after, start)
+        deliver_kernel,
+        in_specs=[hbm] * n,
+        out_specs=[hbm] * n,
+        out_shape=[jax.ShapeDtypeStruct(a.shape, a.dtype) for a in arrays],
+        scratch_shapes=[pltpu.VMEM(a.shape, a.dtype) for a in arrays]
+        + [pltpu.SemaphoreType.DMA((n,))] * 2,
+        compiler_params=pltpu.CompilerParams(vmem_limit_bytes=60 * 2**20),
+        name="deliver",
+    )(*arrays)
 
 
 def shards(inputs, log_decay, read_in, read_out, initial_state, output_grad):
     n_outer, n_inner = lax.axis_size("outer"), lax.axis_size("inner")
-    own_heads, width, depth = initial_state.shape
-    heads = own_heads * n_inner
+    width, depth = initial_state.shape[1:]
     decay = log_decay.T
-    tokens = (inputs, decay, read_in, read_out, output_grad)
-    state, after, start = carry(
-        *tokens, initial_state.reshape(-1, depth), n_outer, n_inner, width, depth
-    )
-    y, dx, ddecay, din, dout, dstart = block(
-        *tokens,
-        state.reshape(-1, depth),
-        after.reshape(-1, depth),
-        start,
-        heads,
+    results = carry(
+        inputs,
+        decay,
+        read_in,
+        read_out,
+        output_grad,
+        initial_state.reshape(-1, depth),
+        n_outer,
+        n_inner,
         width,
         depth,
     )
+    y, dx, ddecay, din, dout, dstart = deliver(*results)
     return (y, dx, ddecay.T, din, dout, dstart.reshape(initial_state.shape))
 
 

time: 88.6 us -> 70.1 us (0.79)
  Pallas kernels: 78.7 us -> 68.6 us
  local copies, waits for them, and re-layouts: 8.79 us -> 0 us
    pallas_call x1, Pallas kernels: 16 us -> 2.99 us  [deliver(): pl.pallas_call(deliver_kernel, in_specs=[hbm] * n, out_specs=[hbm] * n, o...]
    unnamed x18 -> x0, local copies, waits for them, and re-layouts: 8.79 us -> none
    pallas_call x1, Pallas kernels: 62.7 us -> 65.6 us  [carry(): pl.pallas_call(functools.partial(carry_kernel, n_inner, n_low, n_high, ra...]
where the time goes in v3:
time: 70.1 us; the launch traced here: 69.2 us
  Pallas kernels  68.6 us (98%)
    pallas_call x1, Pallas kernels, carry(): pl.pallas_call(functools.partial(carry_kernel, n_inner, n_low, n_high, ra...  65.6 us
    pallas_call x1, Pallas kernels, deliver(): pl.pallas_call(deliver_kernel, in_specs=[hbm] * n, out_specs=[hbm] * n, o...  2.99 us

profile of v3, /device:TPU:0, one launch (start us, length us, event | category | flops | bytes accessed | tf_op | source)
XLA Modules:
  0.0 69.2 jit_solution(10044267651744337599)
XLA Ops:
  0.6 65.6 %carry.1 = (bf16[128,4096]{1,0:T(8,128)(2,1)}, bf16[128,4096]{1,0:T(8,128)(2,1)}, bf16[64,128]{1,0:T(8,128)(2,1)}, bf16[128,1024]{1,0:T(8,128)(2,1)}, bf16[128,1024]{1,0:T(8,128)(2,1)}, /*index=5*/f32[1024,128]{1,0:T(8,128)}) custom-call(bf16[128,4096]{1,0:T(8,128)(2,1)} %x_hbm.1, bf16[64,128]{1,0:T(8,128)(2,1)} %bitcast.5, bf16[128,1024]{1,0:T(8,128)(2,1)} %in_hbm.1, ...), custom_call_target="tpu_custom_call" | custom-call | tf_op jit(solution)/shard_map/carry/pallas_call | solution.py:668
  66.2 3.0 %deliver.1 = (bf16[128,4096]{1,0:T(8,128)(2,1)}, bf16[128,4096]{1,0:T(8,128)(2,1)}, bf16[64,128]{1,0:T(8,128)(2,1)}, bf16[128,1024]{1,0:T(8,128)(2,1)}, bf16[128,1024]{1,0:T(8,128)(2,1)}, /*index=5*/f32[1024,128]{1,0:T(8,128)}) custom-call(bf16[128,4096]{1,0:T(8,128)(2,1)} %get-tuple-element.18.refs_0_, bf16[128,4096]{1,0:T(8,128)(2,1)} %get-tuple-element.19.refs_1_, ...), custom_call_target="tpu_custom_call" | custom-call | tf_op jit(solution)/shard_map/deliver/pallas_call | solution.py:762

commit v4 on v3

--- a/solution.py
+++ b/solution.py
@@ -120,6 +120,8 @@
     before,
     send_behind,
     behind,
+    send_first,
+    firsts,
     send_state,
     send_after,
     load_sem,
@@ -130,6 +132,7 @@
     low_recv,
     high_send,
     high_recv,
+    ready,
 ):
     outer = lax.axis_index("outer")
     inner = lax.axis_index("inner")
@@ -139,14 +142,18 @@
     depth = in_ref.shape[1] * ratio // decay_ref.shape[0]
     columns = ratio * width
 
+    def around(here, k, n):
+        there = here + k
+        return jnp.where(there >= n, there - n, there)
+
     def inner_peer(k):
-        return lax.rem(inner + k, n_inner)
+        return around(inner, k, n_inner)
 
     def low_peer(k):
-        return lax.rem(low + k, n_low)
+        return around(low, k, n_low)
 
     def high_peer(k):
-        return lax.rem(high + k, n_high)
+        return around(high, k, n_high)
 
     def inner_id(k):
         return (outer, inner_peer(k))
@@ -163,6 +170,10 @@
             return none
 
         lax.fori_loop(1, n, body, 0)
+
+    def unrolled(n, act):
+        for k in range(1, n):
+            act(k)
 
     def remote(src, dst, send, recv, to):
         return pltpu.make_async_remote_copy(
@@ -201,6 +212,15 @@
             high_id(k),
         )
 
+    def first_copy(half, k):
+        return remote(
+            send_first.at[half],
+            firsts.at[half, low],
+            low_send.at[9 + half, k],
+            low_recv.at[9 + half, k],
+            low_id(k),
+        )
+
     def total_copy(k):
         return remote(
             send_total.at[inner_peer(k)],
@@ -236,20 +256,19 @@
 
     barrier = pltpu.get_barrier_semaphore()
     for n, peer in ((n_inner, inner_id), (n_low, low_id), (n_high, high_id)):
-        each(
+        unrolled(
             n,
             lambda k, peer=peer: pl.semaphore_signal(
                 barrier, inc=1, device_id=peer(k), device_id_type=MESH
             ),
         )
 
-    totals = dot(decay_ref[...], jnp.ones((length, send_total.shape[2]), BF16), NN)
-    for e in range(n_inner):
-        send_total[e] = totals[e * 2 * ratio : (e + 1) * 2 * ratio]
-
-    pl.semaphore_wait(barrier, n_inner + n_low + n_high - 3)
-    each(n_inner, lambda k: total_copy(k).start())
-    total1[inner] = send_total[inner]
+    def send_totals():
+        totals = dot(decay_ref[...], jnp.ones((length, send_total.shape[2]), BF16), NN)
+        for e in range(n_inner):
+            send_total[e] = totals[e * 2 * ratio : (e + 1) * 2 * ratio]
+        unrolled(n_inner, lambda k: total_copy(k).start())
+        total1[inner] = send_total[inner]
 
     def half_rows(half):
         return pl.ds(half * columns, columns)
@@ -309,7 +328,7 @@
         return as_bf16(iota((columns, heads), 1) == head)
 
     def state_part(half, k):
-        owner = inner_peer(n_inner - k)
+        owner = around(inner, n_inner - k, n_inner)
         group = 2 * owner + half
         wide, narrow = group_slices(group)
         state = state_ref[owner, half_rows(half), :]
@@ -320,8 +339,15 @@
         change = y * grad_ref[:, wide].astype(F32) - x_ref[:, wide].astype(F32) * dx_sum[:, wide]
         up_sum[...] += split_dot(change, place(group), NN)
 
+    def part_stores(half, k):
+        wide, narrow = group_slices(2 * around(inner, n_inner - k, n_inner) + half)
+        return (
+            store(4 + 2 * (half * n_inner + k), dx_ref.at[:, wide], dx_hbm.at[:, wide]),
+            store(5 + 2 * (half * n_inner + k), din_ref.at[:, narrow], din_hbm.at[:, narrow]),
+        )
+
     def after_part(half, k):
-        owner = inner_peer(n_inner - k)
+        owner = around(inner, n_inner - k, n_inner)
         group = 2 * owner + half
         wide, narrow = group_slices(group)
         state = state_ref[owner, half_rows(half), :]
@@ -337,6 +363,8 @@
         state_sum[pl.ds(pl.multiple_of(group * ratio, ratio), ratio), :] = jnp.sum(
             product.reshape(ratio, width, depth), axis=1
         ) * jnp.exp(total)
+        for copy in part_stores(half, k):
+            copy.start()
 
     def local_parts(start, stop):
         def body(group, none):
@@ -358,12 +386,13 @@
     def store(i, src, dst):
         return pltpu.make_async_copy(src, dst, store_sem.at[i])
 
-    def send_gains(half):
+    def fill_gains(half, go):
         at = half_rows(half)
 
         def act(k):
             send_gain[inner_peer(k), at, :] = gain_of(half, k)
-            inner_copy(1 + half, k, send_gain, gain1, at).start()
+            if go:
+                inner_copy(1 + half, k, send_gain, gain1, at).start()
 
         each(n_inner, act)
         gain1[inner, at, :] = gain_of(half, 0)
@@ -378,37 +407,37 @@
         own1[inner, at, :] = own_of(half, 0)
 
     def send_inner(stage, src, dst, half):
-        each(n_inner, lambda k: inner_copy(stage + half, k, src, dst, half_rows(half)).start())
+        unrolled(n_inner, lambda k: inner_copy(stage + half, k, src, dst, half_rows(half)).start())
 
     def recv_inner(stage, src, dst, half):
-        each(n_inner, lambda k: inner_copy(stage + half, k, src, dst, half_rows(half)).wait_recv())
+        unrolled(n_inner, lambda k: inner_copy(stage + half, k, src, dst, half_rows(half)).wait_recv())
 
     def sent_inner(stage, src, dst, half):
-        each(n_inner, lambda k: inner_copy(stage + half, k, src, dst, half_rows(half)).wait_send())
+        unrolled(n_inner, lambda k: inner_copy(stage + half, k, src, dst, half_rows(half)).wait_send())
 
     def keep_inner(src, dst, half):
         at = half_rows(half)
         dst[inner, at, :] = src[inner, at, :]
 
     def send_low(stage, src, dst, half):
-        each(n_low, lambda k: low_copy(stage + half, k, src, dst, half).start())
+        unrolled(n_low, lambda k: low_copy(stage + half, k, src, dst, half).start())
         dst[half, low] = src[half, low]
 
     def recv_low(stage, src, dst, half):
-        each(n_low, lambda k: low_copy(stage + half, k, src, dst, half).wait_recv())
+        unrolled(n_low, lambda k: low_copy(stage + half, k, src, dst, half).wait_recv())
 
     def sent_low(stage, src, dst, half):
-        each(n_low, lambda k: low_copy(stage + half, k, src, dst, half).wait_send())
+        unrolled(n_low, lambda k: low_copy(stage + half, k, src, dst, half).wait_send())
 
     def send_high(stage, src, dst, half):
-        each(n_high, lambda k: high_copy(stage + half, k, src, dst, half).start())
+        unrolled(n_high, lambda k: high_copy(stage + half, k, src, dst, half).start())
         dst[half, high] = src[half]
 
     def recv_high(stage, src, dst, half):
-        each(n_high, lambda k: high_copy(stage + half, k, src, dst, half).wait_recv())
+        unrolled(n_high, lambda k: high_copy(stage + half, k, src, dst, half).wait_recv())
 
     def sent_high(stage, src, dst, half):
-        each(n_high, lambda k: high_copy(stage + half, k, src, dst, half).wait_send())
+        unrolled(n_high, lambda k: high_copy(stage + half, k, src, dst, half).wait_send())
 
     def factor1(e, head):
         return jnp.exp(total1[e, pl.ds(head, 1), :])
@@ -474,10 +503,9 @@
         for e in range(n_high - 1, -1, -1):
             first = factor3(e, half) * first + own3[half, e].astype(F32)
             value = jnp.where(e > high, first, value)
-        first = first.astype(BF16)
+        send_first[half] = first.astype(BF16)
         for e in range(n_low - 1, -1, -1):
-            send_behind[half, e, 0:width] = value.astype(BF16)
-            send_behind[half, e, width:] = first
+            send_behind[half, e] = value.astype(BF16)
             if e > 0:
                 value = factor2(e, half) * value + own2[half, e].astype(F32)
 
@@ -499,8 +527,7 @@
         def body(r, none):
             head = half * ratio + r
             at = head_rows(head)
-            start_ref[at, :] = behind[half, r, width:].astype(F32)
-            value = behind[half, r, 0:width].astype(F32)
+            value = behind[half, r].astype(F32)
             for e in range(n_inner - 1, -1, -1):
                 send_after[e, at, :] = value.astype(BF16)
                 if e > 0:
@@ -510,138 +537,151 @@
         lax.fori_loop(0, ratio, body, 0)
         keep_inner(send_after, after_ref, half)
 
+    def send_firsts(half):
+        unrolled(n_low, lambda k: first_copy(half, k).start())
+        firsts[half, low] = send_first[half]
+
+    def put_firsts(half):
+        unrolled(n_low, lambda k: first_copy(half, k).wait_recv())
+        for r in range(ratio):
+            start_ref[pl.ds((half * ratio + r) * width, width), :] = firsts[half, r].astype(F32)
+
     gains, owns = (1, send_gain, gain1), (3, send_own, own1)
     states, afters = (5, send_state, state_ref), (7, send_after, after_ref)
     gains2, owns2 = (1, send_gain2, gain2), (3, send_own2, own2)
     befores, behinds = (5, send_before, before), (7, send_behind, behind)
     gains3, owns3 = (1, send_gain3, gain3), (3, send_own3, own3)
 
+    up_sum[...] = jnp.zeros_like(up_sum)
+    low_sum[...] = jnp.zeros_like(low_sum)
     loads[0].wait()
     loads[1].wait()
-    send_gains(0)
-    send_gains(1)
-
-    each(n_inner, lambda k: total_copy(k).wait_recv())
+    fill_gains(0, False)
+    pl.semaphore_wait(barrier, n_inner + n_low + n_high - 3)
+    send_totals()
+    send_inner(*gains, 0)
+    fill_gains(1, True)
+    loads[2].wait()
+    loads[3].wait()
+    fill_owns(0)
+
+    unrolled(n_inner, lambda k: total_copy(k).wait_recv())
     row = total1[0]
     for e in range(1, n_inner):
         row = row + total1[e]
     send_total2[...] = row
-    each(n_low, lambda k: total2_copy(k).start())
     total2[low] = row
-
-    loads[2].wait()
-    loads[3].wait()
-    fill_owns(0)
+    unrolled(n_low, lambda k: total2_copy(k).start())
     fill_owns(1)
-
-    each(n_low, lambda k: total2_copy(k).wait_recv())
+    local_parts(0, 2)
+
+    unrolled(n_low, lambda k: total2_copy(k).wait_recv())
     row = total2[0]
     for e in range(1, n_low):
         row = row + total2[e]
     send_total3[...] = row
-    each(n_high, lambda k: total3_copy(k).start())
     total3[high] = row
-
-    up_sum[...] = jnp.zeros_like(up_sum)
-    low_sum[...] = jnp.zeros_like(low_sum)
-
+    unrolled(n_high, lambda k: total3_copy(k).start())
     recv_inner(*gains, 0)
     fold_gains(0)
     send_low(*gains2, 0)
-    local_parts(0, 1)
+    send_inner(*owns, 0)
+    local_parts(2, 6)
     recv_low(*gains2, 0)
     fold_gains2(0)
     send_high(*gains3, 0)
-    sent_inner(*gains, 0)
-    sent_inner(*gains, 1)
-    send_inner(*owns, 0)
-    each(n_high, lambda k: total3_copy(k).wait_recv())
-    loads[4].wait()
-    loads[5].wait()
     recv_inner(*gains, 1)
     fold_gains(1)
     send_low(*gains2, 1)
+    send_inner(*owns, 1)
+    local_parts(6, 8)
+    loads[4].wait()
+    loads[5].wait()
+    unrolled(n_high, lambda k: total3_copy(k).wait_recv())
     recv_high(*gains3, 0)
     spread_states(0)
     send_low(*befores, 0)
-    local_parts(1, 2)
     recv_low(*gains2, 1)
     fold_gains2(1)
     send_high(*gains3, 1)
-    sent_inner(*owns, 0)
-    send_inner(*owns, 1)
-    recv_high(*gains3, 1)
-    spread_states(1)
-    send_low(*befores, 1)
     recv_inner(*owns, 0)
     fold_owns(0)
     send_low(*owns2, 0)
     recv_low(*befores, 0)
     fill_states(0)
+    send_inner(*states, 0)
+    recv_high(*gains3, 1)
+    spread_states(1)
+    send_low(*befores, 1)
     recv_low(*owns2, 0)
     fold_owns2(0)
     send_high(*owns3, 0)
-    recv_low(*befores, 1)
-    fill_states(1)
-    sent_inner(*owns, 1)
-    send_inner(*states, 0)
     recv_inner(*owns, 1)
     fold_owns(1)
     send_low(*owns2, 1)
+    recv_low(*befores, 1)
+    fill_states(1)
+    send_inner(*states, 1)
     recv_high(*owns3, 0)
     spread_afters(0)
     send_low(*behinds, 0)
-    local_parts(2, 3)
+    send_firsts(0)
     recv_low(*owns2, 1)
     fold_owns2(1)
     send_high(*owns3, 1)
-    sent_inner(*states, 0)
-    send_inner(*states, 1)
+    parts(states, 0, state_part)
+    recv_low(*behinds, 0)
+    fill_afters(0)
+    send_inner(*afters, 0)
     recv_high(*owns3, 1)
     spread_afters(1)
     send_low(*behinds, 1)
-    recv_low(*behinds, 0)
-    fill_afters(0)
-    local_parts(3, 6)
-    sent_inner(*states, 1)
-    send_inner(*afters, 0)
+    send_firsts(1)
+    parts(states, 1, state_part)
     recv_low(*behinds, 1)
     fill_afters(1)
+    send_inner(*afters, 1)
+    put_firsts(0)
+    put_firsts(1)
+    for half in range(2):
+        unrolled(n_low, lambda k, half=half: first_copy(half, k).wait_send())
     store_start = store(0, start_ref, dstart_hbm)
     store_start.start()
-    local_parts(6, 8)
-    parts(states, 0, state_part)
-    sent_inner(*afters, 0)
-    send_inner(*afters, 1)
-    parts(states, 1, state_part)
     stores = [store(1, y_ref, y_hbm), store(2, dout_ref, dout_hbm)]
     for copy in stores:
         copy.start()
 
-    each(n_inner, lambda k: total_copy(k).wait_send())
-    each(n_low, lambda k: total2_copy(k).wait_send())
-    each(n_high, lambda k: total3_copy(k).wait_send())
+    unrolled(n_inner, lambda k: total_copy(k).wait_send())
+    unrolled(n_low, lambda k: total2_copy(k).wait_send())
+    unrolled(n_high, lambda k: total3_copy(k).wait_send())
     for half in range(2):
         for stage in (gains2, owns2, befores, behinds):
             sent_low(*stage, half)
         for stage in (gains3, owns3):
             sent_high(*stage, half)
-    parts(afters, 0, after_part)
-    sent_inner(*afters, 1)
-    parts(afters, 1, after_part)
-
+        for stage in (gains, owns, states):
+            sent_inner(*stage, half)
     row = iota((length, length), 0)
     column = iota((length, length), 1)
+    up_total = exact_dot(up_sum[...], jnp.where(row >= column, 1.0, 0.0), TN)
+    parts(afters, 0, after_part)
+    parts(afters, 1, after_part)
+    sent_inner(*afters, 0)
+    sent_inner(*afters, 1)
+
     ddecay_ref[...] = (
-        exact_dot(up_sum[...], jnp.where(row >= column, 1.0, 0.0), TN)
+        up_total
         + exact_dot(low_sum[...], jnp.where(row < column, 1.0, 0.0), TN)
         + jnp.sum(state_sum[...], axis=1, keepdims=True)
     ).astype(BF16)
-    ends = [store(3, dx_ref, dx_hbm), store(4, din_ref, din_hbm), store(5, ddecay_ref, ddecay_hbm)]
-    for copy in ends:
-        copy.start()
-    for copy in [store_start] + stores + ends:
+    end = store(3, ddecay_ref, ddecay_hbm)
+    end.start()
+    for copy in [store_start] + stores + [end]:
         copy.wait()
+    for half in range(2):
+        for k in range(n_inner):
+            for copy in part_stores(half, k):
+                copy.wait()
 
 
 def carry(x, decay, read_in, read_out, grad, init, n_outer, n_inner, width, depth):
@@ -656,7 +696,6 @@
     hbm = pl.BlockSpec(memory_space=pl.ANY)
     chunks = pltpu.VMEM((n_inner, mine * width, depth), BF16)
     runs = pltpu.VMEM((2, n_low, width, depth), BF16)
-    doubles = pltpu.VMEM((2, n_low, 2 * width, depth), BF16)
     head = pltpu.VMEM((2, width, depth), BF16)
     highs = pltpu.VMEM((2, n_high, width, depth), BF16)
     total = pltpu.VMEM((mine, depth), F32)
@@ -722,18 +761,21 @@
             highs,
             runs,
             runs,
-            doubles,
-            doubles,
+            runs,
+            runs,
+            head,
+            runs,
             chunks,
             chunks,
             dma((6,)),
-            dma((6,)),
+            dma((4 + 4 * n_inner,)),
             dma((9, n_inner)),
             dma((9, n_inner)),
-            dma((9, n_low)),
-            dma((9, n_low)),
+            dma((11, n_low)),
+            dma((11, n_low)),
             dma((5, n_high)),
             dma((5, n_high)),
+            pltpu.SemaphoreType.REGULAR((2,)),
         ],
         compiler_params=pltpu.CompilerParams(
             collective_id=0, has_side_effects=True, vmem_limit_bytes=60 * 2**20

time: 70.1 us -> 65.6 us (0.936)
  Pallas kernels: 68.6 us -> 64 us
    pallas_call x1, Pallas kernels: 65.6 us -> 61.1 us  [carry(): pl.pallas_call(functools.partial(carry_kernel, n_inner, n_low, n_high, ra...]
where the time goes in v4:
time: 65.6 us; the launch traced here: 64.7 us
  Pallas kernels  64 us (98%)
    pallas_call x1, Pallas kernels, carry(): pl.pallas_call(functools.partial(carry_kernel, n_inner, n_low, n_high, ra...  61.1 us
    pallas_call x1, Pallas kernels, deliver(): pl.pallas_call(deliver_kernel, in_specs=[hbm] * n, out_specs=[hbm] * n, o...  2.99 us

profile of v4, /device:TPU:0, one launch (start us, length us, event | category | flops | bytes accessed | tf_op | source)
XLA Modules:
  0.0 64.7 jit_solution(2021829834219244521)
XLA Ops:
  0.6 61.1 %carry.1 = (bf16[128,4096]{1,0:T(8,128)(2,1)}, bf16[128,4096]{1,0:T(8,128)(2,1)}, bf16[64,128]{1,0:T(8,128)(2,1)}, bf16[128,1024]{1,0:T(8,128)(2,1)}, bf16[128,1024]{1,0:T(8,128)(2,1)}, /*index=5*/f32[1024,128]{1,0:T(8,128)}) custom-call(bf16[128,4096]{1,0:T(8,128)(2,1)} %x_hbm.1, bf16[64,128]{1,0:T(8,128)(2,1)} %bitcast.5, bf16[128,1024]{1,0:T(8,128)(2,1)} %in_hbm.1, ...), custom_call_target="tpu_custom_call" | custom-call | tf_op jit(solution)/shard_map/carry/pallas_call | solution.py:707
  61.7 3.0 %deliver.1 = (bf16[128,4096]{1,0:T(8,128)(2,1)}, bf16[128,4096]{1,0:T(8,128)(2,1)}, bf16[64,128]{1,0:T(8,128)(2,1)}, bf16[128,1024]{1,0:T(8,128)(2,1)}, bf16[128,1024]{1,0:T(8,128)(2,1)}, /*index=5*/f32[1024,128]{1,0:T(8,128)}) custom-call(bf16[128,4096]{1,0:T(8,128)(2,1)} %get-tuple-element.18.refs_0_, bf16[128,4096]{1,0:T(8,128)(2,1)} %get-tuple-element.19.refs_1_, ...), custom_call_target="tpu_custom_call" | custom-call | tf_op jit(solution)/shard_map/deliver/pallas_call | solution.py:804

commit v5 on v4

--- a/solution.py
+++ b/solution.py
@@ -172,7 +172,7 @@
         lax.fori_loop(1, n, body, 0)
 
     def unrolled(n, act):
-        for k in range(1, n):
+        for k in sorted(range(1, n), key=lambda k: -min(k, n - k)):
             act(k)
 
     def remote(src, dst, send, recv, to):
@@ -240,19 +240,40 @@
             send_total3, total3.at[high], high_send.at[0, k], high_recv.at[0, k], high_id(k)
         )
 
-    loads = [
-        pltpu.make_async_copy(src, dst, load_sem.at[i])
-        for i, (src, dst) in enumerate(
-            ((x_hbm, x_ref), (in_hbm, in_ref), (grad_hbm, grad_ref), (out_hbm, out_ref))
-        )
-    ]
+    def group_slices(group):
+        return (
+            pl.ds(pl.multiple_of(group * columns, columns), columns),
+            pl.ds(pl.multiple_of(group * depth, depth), depth),
+        )
+
+    ORDER = sorted(range(1, n_inner), key=lambda k: -min(k, n_inner - k))
+
+    def x_load(half, k):
+        wide = group_slices(2 * inner_peer(k) + half)[0]
+        return pltpu.make_async_copy(
+            x_hbm.at[:, wide], x_ref.at[:, wide], load_sem.at[5 + half * n_inner + k]
+        )
+
+    def load(i, src, dst):
+        return pltpu.make_async_copy(src, dst, load_sem.at[i])
+
+    def init_load(half):
+        rows = pl.ds(pl.multiple_of((half * ratio + low) * width, width), width)
+        return load(half, init_hbm.at[rows], init_ref.at[half])
+
+    load_in, load_grad, load_out = (
+        load(2, in_hbm, in_ref),
+        load(3, grad_hbm, grad_ref),
+        load(4, out_hbm, out_ref),
+    )
+    load_in.start()
     for half in range(2):
-        rows = pl.ds(pl.multiple_of((half * ratio + low) * width, width), width)
-        loads.append(
-            pltpu.make_async_copy(init_hbm.at[rows], init_ref.at[half], load_sem.at[4 + half])
-        )
-    for load in loads:
-        load.start()
+        for k in ORDER + [0]:
+            x_load(half, k).start()
+    load_grad.start()
+    load_out.start()
+    init_load(0).start()
+    init_load(1).start()
 
     barrier = pltpu.get_barrier_semaphore()
     for n, peer in ((n_inner, inner_id), (n_low, low_id), (n_high, high_id)):
@@ -273,15 +294,10 @@
     def half_rows(half):
         return pl.ds(half * columns, columns)
 
-    def group_slices(group):
-        return (
-            pl.ds(pl.multiple_of(group * columns, columns), columns),
-            pl.ds(pl.multiple_of(group * depth, depth), depth),
-        )
-
     def gain_of(half, k):
         group = 2 * inner_peer(k) + half
         wide, narrow = group_slices(group)
+        x_load(half, k).wait()
         summed = spread_sums(decay_ref, group, ratio, width)
         from_start[:, wide] = jnp.exp(summed)
         factor = jnp.exp(summed[length - 1 :] - summed)
@@ -376,26 +392,21 @@
 
     def parts(stage, half, part):
         part(half, 0)
-
-        def act(k):
+        for k in ORDER:
             inner_copy(stage[0] + half, k, stage[1], stage[2], half_rows(half)).wait_recv()
             part(half, k)
 
-        each(n_inner, act)
-
     def store(i, src, dst):
         return pltpu.make_async_copy(src, dst, store_sem.at[i])
 
-    def fill_gains(half, go):
-        at = half_rows(half)
-
-        def act(k):
-            send_gain[inner_peer(k), at, :] = gain_of(half, k)
-            if go:
-                inner_copy(1 + half, k, send_gain, gain1, at).start()
-
-        each(n_inner, act)
-        gain1[inner, at, :] = gain_of(half, 0)
+    def fill_gain(half, k):
+        send_gain[inner_peer(k), half_rows(half), :] = gain_of(half, k)
+
+    def send_gains(half, start):
+        for k in ORDER[start:]:
+            fill_gain(half, k)
+            inner_copy(1 + half, k, send_gain, gain1, half_rows(half)).start()
+        gain1[inner, half_rows(half), :] = gain_of(half, 0)
 
     def fill_owns(half):
         at = half_rows(half)
@@ -407,7 +418,8 @@
         own1[inner, at, :] = own_of(half, 0)
 
     def send_inner(stage, src, dst, half):
-        unrolled(n_inner, lambda k: inner_copy(stage + half, k, src, dst, half_rows(half)).start())
+        for k in ORDER:
+            inner_copy(stage + half, k, src, dst, half_rows(half)).start()
 
     def recv_inner(stage, src, dst, half):
         unrolled(n_inner, lambda k: inner_copy(stage + half, k, src, dst, half_rows(half)).wait_recv())
@@ -461,7 +473,7 @@
             send_gain2[half, r] = value.astype(BF16)
             return none
 
-        lax.fori_loop(0, ratio, body, 0)
+        lax.fori_loop(0, ratio, body, 0, unroll=4)
 
     def fold_owns(half):
         def body(r, none):
@@ -473,7 +485,7 @@
             send_own2[half, r] = value.astype(BF16)
             return none
 
-        lax.fori_loop(0, ratio, body, 0)
+        lax.fori_loop(0, ratio, body, 0, unroll=4)
 
     def fold_gains2(half):
         value = gain2[half, 0].astype(F32)
@@ -520,7 +532,7 @@
                     value = factor1(e, head) * value + gain1[e, at, :].astype(F32)
             return none
 
-        lax.fori_loop(0, ratio, body, 0)
+        lax.fori_loop(0, ratio, body, 0, unroll=4)
         keep_inner(send_state, state_ref, half)
 
     def fill_afters(half):
@@ -534,7 +546,7 @@
                     value = factor1(e, head) * value + own1[e, at, :].astype(F32)
             return none
 
-        lax.fori_loop(0, ratio, body, 0)
+        lax.fori_loop(0, ratio, body, 0, unroll=4)
         keep_inner(send_after, after_ref, half)
 
     def send_firsts(half):
@@ -554,15 +566,15 @@
 
     up_sum[...] = jnp.zeros_like(up_sum)
     low_sum[...] = jnp.zeros_like(low_sum)
-    loads[0].wait()
-    loads[1].wait()
-    fill_gains(0, False)
+    load_in.wait()
+    fill_gain(0, ORDER[0])
     pl.semaphore_wait(barrier, n_inner + n_low + n_high - 3)
     send_totals()
-    send_inner(*gains, 0)
-    fill_gains(1, True)
-    loads[2].wait()
-    loads[3].wait()
+    inner_copy(1, ORDER[0], send_gain, gain1, half_rows(0)).start()
+    send_gains(0, 1)
+    send_gains(1, 0)
+    load_grad.wait()
+    load_out.wait()
     fill_owns(0)
 
     unrolled(n_inner, lambda k: total_copy(k).wait_recv())
@@ -595,8 +607,8 @@
     send_low(*gains2, 1)
     send_inner(*owns, 1)
     local_parts(6, 8)
-    loads[4].wait()
-    loads[5].wait()
+    init_load(0).wait()
+    init_load(1).wait()
     unrolled(n_high, lambda k: total3_copy(k).wait_recv())
     recv_high(*gains3, 0)
     spread_states(0)
@@ -767,7 +779,7 @@
             runs,
             chunks,
             chunks,
-            dma((6,)),
+            dma((5 + 2 * n_inner,)),
             dma((4 + 4 * n_inner,)),
             dma((9, n_inner)),
             dma((9, n_inner)),
@@ -784,11 +796,20 @@
     )(x, decay, read_in, read_out, grad, init)
 
 
-def deliver_kernel(*refs):
-    n = (len(refs) - 2) // 3
+def deliver_kernel(parts, *refs):
+    n = len(parts)
     hbm, out, held, (loaded, stored) = refs[:n], refs[n : 2 * n], refs[2 * n : 3 * n], refs[3 * n :]
-    loads = [pltpu.make_async_copy(hbm[i], held[i], loaded.at[i]) for i in range(n)]
-    stores = [pltpu.make_async_copy(held[i], out[i], stored.at[i]) for i in range(n)]
+    loads, stores = [], []
+    for i, part in enumerate(parts):
+        rows = hbm[i].shape[0] // part
+        for p in range(part):
+            at, sem = pl.ds(p * rows, rows), len(loads)
+            loads.append(
+                pltpu.make_async_copy(hbm[i].at[at], held[i].at[at], loaded.at[sem])
+            )
+            stores.append(
+                pltpu.make_async_copy(held[i].at[at], out[i].at[at], stored.at[sem])
+            )
     for load in loads:
         load.start()
     for load, store in zip(loads, stores):
@@ -801,13 +822,14 @@
 def deliver(*arrays):
     n = len(arrays)
     hbm = pl.BlockSpec(memory_space=pl.ANY)
+    parts = [4 if a.size >= 2**19 else 1 for a in arrays]
     return pl.pallas_call(
-        deliver_kernel,
+        functools.partial(deliver_kernel, parts),
         in_specs=[hbm] * n,
         out_specs=[hbm] * n,
         out_shape=[jax.ShapeDtypeStruct(a.shape, a.dtype) for a in arrays],
         scratch_shapes=[pltpu.VMEM(a.shape, a.dtype) for a in arrays]
-        + [pltpu.SemaphoreType.DMA((n,))] * 2,
+        + [pltpu.SemaphoreType.DMA((sum(parts),))] * 2,
         compiler_params=pltpu.CompilerParams(vmem_limit_bytes=60 * 2**20),
         name="deliver",
     )(*arrays)

time: 65.6 us -> 64.3 us (0.980)
  Pallas kernels: 64 us -> 62.5 us
    pallas_call x1, Pallas kernels: 61.1 us -> 59.6 us  [carry(): pl.pallas_call(functools.partial(carry_kernel, n_inner, n_low, n_high, ra...]
where the time goes in v5:
time: 64.3 us; the launch traced here: 63.3 us
  Pallas kernels  62.5 us (97%)
  between operations  0.8 us (1%)
    pallas_call x1, Pallas kernels, carry(): pl.pallas_call(functools.partial(carry_kernel, n_inner, n_low, n_high, ra...  59.6 us
    pallas_call x1, Pallas kernels, deliver(): pl.pallas_call(functools.partial(deliver_kernel, parts), in_specs=[hbm] *...  2.85 us

profile of v5, /device:TPU:0, one launch (start us, length us, event | category | flops | bytes accessed | tf_op | source)
XLA Modules:
  0.0 63.3 jit_solution(4163604688880402886)
XLA Ops:
  0.6 59.6 %carry.1 = (bf16[128,4096]{1,0:T(8,128)(2,1)}, bf16[128,4096]{1,0:T(8,128)(2,1)}, bf16[64,128]{1,0:T(8,128)(2,1)}, bf16[128,1024]{1,0:T(8,128)(2,1)}, bf16[128,1024]{1,0:T(8,128)(2,1)}, /*index=5*/f32[1024,128]{1,0:T(8,128)}) custom-call(bf16[128,4096]{1,0:T(8,128)(2,1)} %x_hbm.1, bf16[64,128]{1,0:T(8,128)(2,1)} %bitcast.5, bf16[128,1024]{1,0:T(8,128)(2,1)} %in_hbm.1, ...), custom_call_target="tpu_custom_call" | custom-call | tf_op jit(solution)/shard_map/carry/pallas_call | solution.py:719
  60.3 2.8 %deliver.1 = (bf16[128,4096]{1,0:T(8,128)(2,1)}, bf16[128,4096]{1,0:T(8,128)(2,1)}, bf16[64,128]{1,0:T(8,128)(2,1)}, bf16[128,1024]{1,0:T(8,128)(2,1)}, bf16[128,1024]{1,0:T(8,128)(2,1)}, /*index=5*/f32[1024,128]{1,0:T(8,128)}) custom-call(bf16[128,4096]{1,0:T(8,128)(2,1)} %get-tuple-element.18.refs_0_, bf16[128,4096]{1,0:T(8,128)(2,1)} %get-tuple-element.19.refs_1_, ...), custom_call_target="tpu_custom_call" | custom-call | tf_op jit(solution)/shard_map/deliver/pallas_call | solution.py:826

commit v6 on v5

--- a/solution.py
+++ b/solution.py
@@ -464,28 +464,36 @@
         return pl.ds(pl.multiple_of(head * width, width), width)
 
     def fold_gains(half):
-        def body(r, none):
+        def fold(r):
             head = half * ratio + r
             at = head_rows(head)
             value = gain1[0, at, :].astype(F32)
             for e in range(1, n_inner):
                 value = factor1(e, head) * value + gain1[e, at, :].astype(F32)
-            send_gain2[half, r] = value.astype(BF16)
-            return none
-
-        lax.fori_loop(0, ratio, body, 0, unroll=4)
+            return value.astype(BF16)
+
+        def act(k):
+            send_gain2[half, low_peer(k)] = fold(low_peer(k))
+            low_copy(1 + half, k, send_gain2, gain2, half).start()
+
+        unrolled(n_low, act)
+        gain2[half, low] = fold(low)
 
     def fold_owns(half):
-        def body(r, none):
+        def fold(r):
             head = half * ratio + r
             at = head_rows(head)
             value = own1[n_inner - 1, at, :].astype(F32)
             for e in range(n_inner - 2, -1, -1):
                 value = factor1(e, head) * value + own1[e, at, :].astype(F32)
-            send_own2[half, r] = value.astype(BF16)
-            return none
-
-        lax.fori_loop(0, ratio, body, 0, unroll=4)
+            return value.astype(BF16)
+
+        def act(k):
+            send_own2[half, low_peer(k)] = fold(low_peer(k))
+            low_copy(3 + half, k, send_own2, own2, half).start()
+
+        unrolled(n_low, act)
+        own2[half, low] = fold(low)
 
     def fold_gains2(half):
         value = gain2[half, 0].astype(F32)
@@ -596,7 +604,6 @@
     unrolled(n_high, lambda k: total3_copy(k).start())
     recv_inner(*gains, 0)
     fold_gains(0)
-    send_low(*gains2, 0)
     send_inner(*owns, 0)
     local_parts(2, 6)
     recv_low(*gains2, 0)
@@ -604,7 +611,6 @@
     send_high(*gains3, 0)
     recv_inner(*gains, 1)
     fold_gains(1)
-    send_low(*gains2, 1)
     send_inner(*owns, 1)
     local_parts(6, 8)
     init_load(0).wait()
@@ -618,7 +624,6 @@
     send_high(*gains3, 1)
     recv_inner(*owns, 0)
     fold_owns(0)
-    send_low(*owns2, 0)
     recv_low(*befores, 0)
     fill_states(0)
     send_inner(*states, 0)
@@ -630,14 +635,12 @@
     send_high(*owns3, 0)
     recv_inner(*owns, 1)
     fold_owns(1)
-    send_low(*owns2, 1)
     recv_low(*befores, 1)
     fill_states(1)
     send_inner(*states, 1)
     recv_high(*owns3, 0)
     spread_afters(0)
     send_low(*behinds, 0)
-    send_firsts(0)
     recv_low(*owns2, 1)
     fold_owns2(1)
     send_high(*owns3, 1)
@@ -645,14 +648,15 @@
     recv_low(*behinds, 0)
     fill_afters(0)
     send_inner(*afters, 0)
+    send_firsts(0)
     recv_high(*owns3, 1)
     spread_afters(1)
     send_low(*behinds, 1)
-    send_firsts(1)
     parts(states, 1, state_part)
     recv_low(*behinds, 1)
     fill_afters(1)
     send_inner(*afters, 1)
+    send_firsts(1)
     put_firsts(0)
     put_firsts(1)
     for half in range(2):

time: 64.3 us -> 64.2 us (level)
  no operation moved by 1% of the time
where the time goes in v6:
time: 64.2 us; the launch traced here: 63.2 us
  Pallas kernels  62.4 us (97%)
  between operations  0.8 us (1%)
    pallas_call x1, Pallas kernels, carry(): pl.pallas_call(functools.partial(carry_kernel, n_inner, n_low, n_high, ra...  59.5 us
    pallas_call x1, Pallas kernels, deliver(): pl.pallas_call(functools.partial(deliver_kernel, parts), in_specs=[hbm] *...  2.85 us

profile of v6, /device:TPU:0, one launch (start us, length us, event | category | flops | bytes accessed | tf_op | source)
XLA Modules:
  0.0 63.2 jit_solution(15008541767049035347)
XLA Ops:
  0.6 59.5 %carry.1 = (bf16[128,4096]{1,0:T(8,128)(2,1)}, bf16[128,4096]{1,0:T(8,128)(2,1)}, bf16[64,128]{1,0:T(8,128)(2,1)}, bf16[128,1024]{1,0:T(8,128)(2,1)}, bf16[128,1024]{1,0:T(8,128)(2,1)}, /*index=5*/f32[1024,128]{1,0:T(8,128)}) custom-call(bf16[128,4096]{1,0:T(8,128)(2,1)} %x_hbm.1, bf16[64,128]{1,0:T(8,128)(2,1)} %bitcast.5, bf16[128,1024]{1,0:T(8,128)(2,1)} %in_hbm.1, ...), custom_call_target="tpu_custom_call" | custom-call | tf_op jit(solution)/shard_map/carry/pallas_call | solution.py:723
  60.2 2.8 %deliver.1 = (bf16[128,4096]{1,0:T(8,128)(2,1)}, bf16[128,4096]{1,0:T(8,128)(2,1)}, bf16[64,128]{1,0:T(8,128)(2,1)}, bf16[128,1024]{1,0:T(8,128)(2,1)}, bf16[128,1024]{1,0:T(8,128)(2,1)}, /*index=5*/f32[1024,128]{1,0:T(8,128)}) custom-call(bf16[128,4096]{1,0:T(8,128)(2,1)} %get-tuple-element.18.refs_0_, bf16[128,4096]{1,0:T(8,128)(2,1)} %get-tuple-element.19.refs_1_, ...), custom_call_target="tpu_custom_call" | custom-call | tf_op jit(solution)/shard_map/deliver/pallas_call | solution.py:830

commit v7 on v6

--- a/solution.py
+++ b/solution.py
@@ -530,7 +530,7 @@
                 value = factor2(e, half) * value + own2[half, e].astype(F32)
 
     def fill_states(half):
-        def body(r, none):
+        def fill(r):
             head = half * ratio + r
             at = head_rows(head)
             value = before[half, r].astype(F32)
@@ -538,13 +538,17 @@
                 send_state[e, at, :] = value.astype(BF16)
                 if e < n_inner - 1:
                     value = factor1(e, head) * value + gain1[e, at, :].astype(F32)
-            return none
-
-        lax.fori_loop(0, ratio, body, 0, unroll=4)
+
+        def act(k):
+            low_copy(5 + half, k, send_before, before, half).wait_recv()
+            fill(around(low, n_low - k, n_low))
+
+        fill(low)
+        unrolled(n_low, act)
         keep_inner(send_state, state_ref, half)
 
     def fill_afters(half):
-        def body(r, none):
+        def fill(r):
             head = half * ratio + r
             at = head_rows(head)
             value = behind[half, r].astype(F32)
@@ -552,9 +556,13 @@
                 send_after[e, at, :] = value.astype(BF16)
                 if e > 0:
                     value = factor1(e, head) * value + own1[e, at, :].astype(F32)
-            return none
-
-        lax.fori_loop(0, ratio, body, 0, unroll=4)
+
+        def act(k):
+            low_copy(7 + half, k, send_behind, behind, half).wait_recv()
+            fill(around(low, n_low - k, n_low))
+
+        fill(low)
+        unrolled(n_low, act)
         keep_inner(send_after, after_ref, half)
 
     def send_firsts(half):
@@ -624,7 +632,6 @@
     send_high(*gains3, 1)
     recv_inner(*owns, 0)
     fold_owns(0)
-    recv_low(*befores, 0)
     fill_states(0)
     send_inner(*states, 0)
     recv_high(*gains3, 1)
@@ -635,7 +642,6 @@
     send_high(*owns3, 0)
     recv_inner(*owns, 1)
     fold_owns(1)
-    recv_low(*befores, 1)
     fill_states(1)
     send_inner(*states, 1)
     recv_high(*owns3, 0)
@@ -645,7 +651,6 @@
     fold_owns2(1)
     send_high(*owns3, 1)
     parts(states, 0, state_part)
-    recv_low(*behinds, 0)
     fill_afters(0)
     send_inner(*afters, 0)
     send_firsts(0)
@@ -653,7 +658,6 @@
     spread_afters(1)
     send_low(*behinds, 1)
     parts(states, 1, state_part)
-    recv_low(*behinds, 1)
     fill_afters(1)
     send_inner(*afters, 1)
     send_firsts(1)

time: 64.2 us -> 64.1 us (level)
  no operation moved by 1% of the time
where the time goes in v7:
time: 64.1 us; the launch traced here: 63.1 us
  Pallas kernels  62.3 us (97%)
  between operations  0.8 us (1%)
    pallas_call x1, Pallas kernels, carry(): pl.pallas_call(functools.partial(carry_kernel, n_inner, n_low, n_high, ra...  59.4 us
    pallas_call x1, Pallas kernels, deliver(): pl.pallas_call(functools.partial(deliver_kernel, parts), in_specs=[hbm] *...  2.85 us

profile of v7, /device:TPU:0, one launch (start us, length us, event | category | flops | bytes accessed | tf_op | source)
XLA Modules:
  0.0 63.1 jit_solution(10494747622471017252)
XLA Ops:
  0.6 59.4 %carry.1 = (bf16[128,4096]{1,0:T(8,128)(2,1)}, bf16[128,4096]{1,0:T(8,128)(2,1)}, bf16[64,128]{1,0:T(8,128)(2,1)}, bf16[128,1024]{1,0:T(8,128)(2,1)}, bf16[128,1024]{1,0:T(8,128)(2,1)}, /*index=5*/f32[1024,128]{1,0:T(8,128)}) custom-call(bf16[128,4096]{1,0:T(8,128)(2,1)} %x_hbm.1, bf16[64,128]{1,0:T(8,128)(2,1)} %bitcast.5, bf16[128,1024]{1,0:T(8,128)(2,1)} %in_hbm.1, ...), custom_call_target="tpu_custom_call" | custom-call | tf_op jit(solution)/shard_map/carry/pallas_call | solution.py:727
  60.1 2.8 %deliver.1 = (bf16[128,4096]{1,0:T(8,128)(2,1)}, bf16[128,4096]{1,0:T(8,128)(2,1)}, bf16[64,128]{1,0:T(8,128)(2,1)}, bf16[128,1024]{1,0:T(8,128)(2,1)}, bf16[128,1024]{1,0:T(8,128)(2,1)}, /*index=5*/f32[1024,128]{1,0:T(8,128)}) custom-call(bf16[128,4096]{1,0:T(8,128)(2,1)} %get-tuple-element.18.refs_0_, bf16[128,4096]{1,0:T(8,128)(2,1)} %get-tuple-element.19.refs_1_, ...), custom_call_target="tpu_custom_call" | custom-call | tf_op jit(solution)/shard_map/deliver/pallas_call | solution.py:834
